TPU v7x, 256 devices: a whole 4x4x8 slice. The times are simulated.
256 devices in a mesh: dp: 32 (over x, z_hi, core), shard: 8 (over y, z_lo).
Axes of the slice: x: 4, y: 4, z: 8 (z_hi: 4, z_lo: 2; z = z_hi * 2 + z_lo), core: 2. Of those that a mesh axis runs over, the one named last changes fastest.
Arguments:
- residual_input: bfloat16 [768, 6144], P('dp'), may hold values from -6 to 6
- attention_mixture: bfloat16 [768, 6144], P('dp', 'shard'), may hold values from -6 to 6
- output_gradient: bfloat16 [768, 6144], P('dp'), may hold values from -6 to 6
- norm_gain_vector: float32 [6144], replicated, may hold values from 0.25 to 1.75
- routes: int32 [768, 2], P('dp'), may hold values from 0 to 7, all different within a row; in each aligned block of 24 rows (0 to 23, 24 to 47, ...) at most 12 rows name the same one
- router_weight: float32 [768, 2], P('dp'), may hold values from 0.2 to 1
- gate_weight: bfloat16 [8, 6144, 8192], P('shard', None, 'dp'), may hold values from -0.078125 to 0.078125
- up_weight: bfloat16 [8, 6144, 8192], P('shard', None, 'dp'), may hold values from -0.078125 to 0.078125
- down_weight: bfloat16 [8, 8192, 6144], P('shard', 'dp'), may hold values from -0.0625 to 0.0625
- gate_adapter_first: bfloat16 [8, 6144, 16], P('shard'), may hold values from -0.078125 to 0.078125
- gate_adapter_second: bfloat16 [8, 16, 8192], P('shard', None, 'dp'), may hold values from -1.5 to 1.5
- attention_adapter_first: bfloat16 [6144, 16], P('shard'), may hold values from -0.078125 to 0.078125
- attention_adapter_second: bfloat16 [16, 6144], P(None, 'shard'), may hold values from -1.5 to 1.5
Outputs:
- residual_gradient: bfloat16 [768, 6144], P('dp', 'shard')
- gate_first_gradient: float32 [8, 6144, 16], P('shard')
- gate_second_gradient: float32 [8, 16, 8192], P('shard', None, 'dp')
- attention_first_gradient: float32 [6144, 16], P('shard')
- attention_second_gradient: float32 [16, 6144], P(None, 'shard')
Inputs may be any that keep to these rules, and one draw needn't show every extreme that they name: No expert is named by more than 12 routes of one aligned block of 24 tokens.
All inputs are finite; a program needn't handle non-finite values.
Results may differ from a plain program's by a relative error of at most 0.023.
Values may be sent and summed in bfloat16 or wider, within the bound.
A program may use at most 128 MiB of HBM per device.

v0:
```python
from functools import partial

import jax
import jax.numpy as jnp
from jax import lax
from jax.sharding import PartitionSpec as P

CAP = 12


EPSILON = 1e-05
ADAPTER_SCALE = 0.5


def norm_rows(hidden, gain):
    wide = hidden.astype(jnp.float32)
    radius = lax.rsqrt(jnp.mean(wide * wide, axis=1) + EPSILON)
    return (radius, (wide * radius[:, None] * gain).astype(jnp.bfloat16))


def slot_table(route_block, expert_ids, capacity):
    flat = route_block.reshape(-1)
    count = flat.shape[0]
    same = (flat[:, None] == flat[None, :]).astype(jnp.int32)
    earlier = (
        jnp.arange(count, dtype=jnp.int32)[:, None] > jnp.arange(count, dtype=jnp.int32)[None, :]
    ).astype(jnp.int32)
    slot = jnp.sum(same * earlier, axis=1)
    match = (flat[None, None, :] == expert_ids[:, None, None]) & (
        slot[None, None, :] == jnp.arange(capacity, dtype=jnp.int32)[None, :, None]
    )
    return match.astype(jnp.float32).reshape(expert_ids.shape[0], capacity, count // 2, 2)


def expert_forward_back(inputs):
    input_rows, rows_dy, gate_matrix, up_w, down_w, adapt_a, adapter_second = inputs
    lowrank_product = jnp.dot(input_rows, adapt_a, preferred_element_type=jnp.float32).astype(
        jnp.bfloat16
    )
    gate_values = jnp.dot(
        input_rows, gate_matrix, preferred_element_type=jnp.float32
    ) + ADAPTER_SCALE * jnp.dot(lowrank_product, adapter_second, preferred_element_type=jnp.float32)
    upper = jnp.dot(input_rows, up_w, preferred_element_type=jnp.float32)
    dact = jnp.dot(rows_dy, down_w.T, preferred_element_type=jnp.float32)
    sigm = jax.nn.sigmoid(gate_values)
    gate_cotangent = (dact * upper * sigm * (1.0 + gate_values * (1.0 - sigm))).astype(jnp.bfloat16)
    dup = (dact * gate_values * sigm).astype(jnp.bfloat16)
    backward_result = ADAPTER_SCALE * jnp.dot(
        gate_cotangent, adapter_second.T, preferred_element_type=jnp.float32
    )
    grad_a = jnp.dot(
        input_rows.astype(jnp.float32).T, backward_result, precision=lax.Precision.HIGHEST
    )
    second_factor = ADAPTER_SCALE * jnp.dot(
        lowrank_product.T, gate_cotangent, preferred_element_type=jnp.float32
    )
    return (gate_cotangent, dup, backward_result, grad_a, second_factor)


def row_term(inputs):
    part_gate, part_up, partial_backward, gate_matrix, up_w, adapt_a = inputs
    term = jnp.dot(part_gate, gate_matrix.T, preferred_element_type=jnp.float32) + jnp.dot(
        part_up, up_w.T, preferred_element_type=jnp.float32
    )
    return term + jnp.dot(
        partial_backward, adapt_a.astype(jnp.float32).T, precision=lax.Precision.HIGHEST
    )


def body(
    residual_input,
    attention_mixture,
    output_gradient,
    norm_gain_vector,
    routes,
    router_weight,
    gate_weight,
    up_weight,
    down_weight,
    gate_adapter_first,
    gate_adapter_second,
    attention_adapter_first,
    attention_adapter_second,
):
    rows_here = residual_input.shape[0]
    width = residual_input.shape[1]
    per_dev = gate_weight.shape[0]
    hidden_part = gate_weight.shape[2]
    rank_count = gate_adapter_first.shape[2]
    slice_width = attention_mixture.shape[1]
    dp_count = lax.axis_size("dp")
    shard_count = lax.axis_size("shard")
    shard_index = lax.axis_index("shard")
    expert_ids = shard_index * per_dev + jnp.arange(per_dev, dtype=jnp.int32)
    radius, normed = norm_rows(residual_input, norm_gain_vector)
    match = slot_table(routes, expert_ids, CAP)
    chooser = jnp.sum(match, axis=3)
    weighted = jnp.sum(match * router_weight[None, None], axis=3)
    packed_input_rows = jnp.einsum(
        "ecT,Td->ecd", chooser, normed.astype(jnp.float32), precision=lax.Precision.HIGHEST
    )
    packed_input_rows = packed_input_rows.astype(jnp.bfloat16).reshape(per_dev * CAP, width)
    packed_output_gradient = jnp.einsum(
        "ecT,Td->ecd",
        weighted,
        output_gradient.astype(jnp.float32),
        precision=lax.Precision.HIGHEST,
    )
    packed_output_gradient = packed_output_gradient.astype(jnp.bfloat16).reshape(
        per_dev * CAP, width
    )
    gathered_x, gathered_dy = (
        lax.all_gather(packed_input_rows, "dp", axis=0, tiled=True),
        lax.all_gather(packed_output_gradient, "dp", axis=0, tiled=True),
    )
    expert_x = jnp.swapaxes(gathered_x.reshape(dp_count, per_dev, CAP, width), 0, 1).reshape(
        per_dev, dp_count * CAP, width
    )
    expert_dy = jnp.swapaxes(gathered_dy.reshape(dp_count, per_dev, CAP, width), 0, 1).reshape(
        per_dev, dp_count * CAP, width
    )
    grads_gate, grads_low, grads_back, grads_a, second_factor_gradients = lax.map(
        expert_forward_back,
        (
            expert_x,
            expert_dy,
            gate_weight,
            up_weight,
            down_weight,
            gate_adapter_first,
            gate_adapter_second,
        ),
    )
    grads_gate = grads_gate.reshape(per_dev, dp_count, CAP, hidden_part)
    grads_low = grads_low.reshape(per_dev, dp_count, CAP, hidden_part)
    grads_back = grads_back.reshape(per_dev, dp_count, CAP, rank_count)
    all_routes = lax.all_gather(routes, "dp", axis=0, tiled=True)
    every_match = jax.vmap(partial(slot_table, expert_ids=expert_ids, capacity=CAP))(
        all_routes.reshape(dp_count, rows_here, 2)
    )
    every_choose = jnp.sum(every_match, axis=4)
    row_count = dp_count * per_dev * CAP
    blocks = row_count // (per_dev * CAP)
    part_gate = grads_gate.reshape(per_dev, blocks * CAP, hidden_part)
    part_up = grads_low.reshape(per_dev, blocks * CAP, hidden_part)
    partial_backward = grads_back.reshape(per_dev, blocks * CAP, rank_count)
    terms = lax.map(
        row_term, (part_gate, part_up, partial_backward, gate_weight, up_weight, gate_adapter_first)
    )
    row_terms = (
        jnp.swapaxes(terms.reshape(per_dev, blocks, CAP, width), 0, 1)
        .reshape(row_count, width)
        .reshape(dp_count, per_dev, CAP, shard_count, slice_width)
    )
    token_term = jnp.einsum(
        "becT,becsd->bsTd", every_choose, row_terms, precision=lax.Precision.HIGHEST
    )
    token_term = token_term.reshape(dp_count * shard_count, rows_here, slice_width)
    grad_norm_in = lax.psum_scatter(
        token_term, ("dp", "shard"), scatter_dimension=0, tiled=True
    ).reshape(rows_here, slice_width)
    offset = shard_index * slice_width
    hidden_slice = lax.dynamic_slice_in_dim(residual_input, offset, slice_width, 1).astype(
        jnp.float32
    )
    grad_slice = lax.dynamic_slice_in_dim(output_gradient, offset, slice_width, 1).astype(
        jnp.float32
    )
    gain_slice = lax.dynamic_slice_in_dim(norm_gain_vector, offset, slice_width, 0)
    spread = gain_slice * grad_norm_in
    stat_part = jnp.sum(spread * hidden_slice, axis=1)
    mixture_partial = jnp.dot(
        attention_mixture, attention_adapter_first, preferred_element_type=jnp.float32
    )
    stat_total, mixed_total = lax.psum((stat_part, mixture_partial), "shard")
    stat = stat_total / width
    residual_gradient = (
        grad_slice + radius[:, None] * spread - hidden_slice * (radius**3 * stat)[:, None]
    ).astype(jnp.bfloat16)
    mixture_lowrank = mixed_total.astype(jnp.bfloat16)
    backward_partial = jnp.dot(
        residual_gradient, attention_adapter_second.T, preferred_element_type=jnp.float32
    )
    backward_lowrank = lax.psum(backward_partial, "shard").astype(jnp.bfloat16)
    first_factor_partial = ADAPTER_SCALE * jnp.dot(
        attention_mixture.T, backward_lowrank, preferred_element_type=jnp.float32
    )
    second_factor_partial = ADAPTER_SCALE * jnp.dot(
        mixture_lowrank.T, residual_gradient, preferred_element_type=jnp.float32
    )
    gate_first_gradient, attention_first_gradient, attention_second_gradient = (
        lax.psum(grads_a.astype(jnp.bfloat16), "dp").astype(jnp.float32),
        lax.psum(first_factor_partial.astype(jnp.bfloat16), "dp").astype(jnp.float32),
        lax.psum(second_factor_partial.astype(jnp.bfloat16), "dp").astype(jnp.float32),
    )
    return (
        residual_gradient,
        gate_first_gradient,
        second_factor_gradients,
        attention_first_gradient,
        attention_second_gradient,
    )


def solution(mesh):
    in_specs = (
        P("dp", None),
        P("dp", "shard"),
        P("dp", None),
        P(),
        P("dp", None),
        P("dp", None),
        P("shard", None, "dp"),
        P("shard", None, "dp"),
        P("shard", "dp", None),
        P("shard", None, None),
        P("shard", None, "dp"),
        P("shard", None),
        P(None, "shard"),
    )
    out_specs = (
        P("dp", "shard"),
        P("shard", None, None),
        P("shard", None, "dp"),
        P("shard", None),
        P(None, "shard"),
    )
    return jax.shard_map(body, mesh=mesh, in_specs=in_specs, out_specs=out_specs, check_vma=False)
```

profile of v0, /device:TPU:1, one launch (start us, length us, event | category | flops | bytes accessed | tf_op | source)
XLA Modules:
  0.0 1949.1 jit_solution(13347982024921784546)
XLA Ops:
  7.2 0.0 copy-start
  7.2 0.0 all-gather.8.cloned.1.call-start
  7.2 1.3 fusion.32
  8.5 0.5 copy-done.12
  9.0 0.8 copy.51
  9.8 0.7 broadcast_compare_fusion.1
  10.5 0.1 eq.114
  10.6 0.2 select_reduce_fusion.1
  10.8 0.1 eq.118
  10.9 0.1 copy.52
  10.9 0.7 convert_reduce_fusion.1
  11.7 2.0 fusion.4
  13.7 0.0 all-gather.8.cloned.1.call-update
  13.7 0.0 all-gather.6.cloned.1.call-start
  13.8 2.0 fusion.3
  15.7 0.0 all-gather.6.cloned.1.call-update
  15.8 0.0 all-reduce.4.cloned.1.call-start
  15.8 49.1 %all-gather.2 = s32[32,24,2]{1,2,0:T(2,128)S(1)} all-gather(s32[1,24,2]{1,2,0:T(2,128)} %bitcast.89), channel_id=1, replica_groups=mesh['dp'=32,'shard'=8] {'dp'}, dimensions={0}, use_global_device_ids=true | all-gather | bytes 6336 | tf_op jit(solution)/shard_map/all_gather | solution.py:137
  64.9 0.1 copy.54
  65.0 0.1 copy.53
  65.1 0.1 copy.55
  65.2 0.8 select_reduce_fusion
  66.0 0.1 copy.57
  66.1 0.1 convert_reduce_fusion
  66.2 0.9 copy.61
  67.1 20.1 %all-gather.8.cloned.1.call-done = bf16[32,12,6144]{2,1,0:T(8,128)(2,1)} async-done(((bf16[1,12,6144]{2,1,0:T(8,128)(2,1)}), bf16[32,12,6144]{2,1,0:T(8,128)(2,1)}) %all-gather.8.cloned.1.call-update) | async-done | bytes 4718608 | tf_op jit(solution)/shard_map/all_gather | solution.py:113
  87.1 7.6 reshape.203
  94.7 3.8 convolution_convert_fusion.3
  98.5 4.2 fusion.7
  102.7 54.1 %all-gather.6.cloned.1.call-done = bf16[32,12,6144]{2,1,0:T(8,128)(2,1)} async-done(((bf16[1,12,6144]{2,1,0:T(8,128)(2,1)}), bf16[32,12,6144]{2,1,0:T(8,128)(2,1)}) %all-gather.6.cloned.1.call-update) | async-done | bytes 4718608 | tf_op jit(solution)/shard_map/all_gather | solution.py:114
  156.8 7.6 reshape.201
  164.4 4.8 fusion.13
  169.2 0.2 fusion.18
  169.5 0.0 slice-start
  169.5 3.9 fusion.25
  173.4 0.0 copy-start.3
  173.4 5.1 fusion.9
  178.5 0.2 convolution_multiply_fusion.3
  178.6 5.1 fusion.5
  183.7 2.6 fusion.2
  186.4 0.0 all-reduce.4.cloned.1.call-update
  186.4 0.2 reduce-scatter.2.cloned.1.call-start
  186.6 10.9 add_add_fusion
  197.5 8.0 copy.64
  205.5 21.2 %fusion = f32[32,8,768,24]{2,3,1,0:T(8,128)} fusion(f32[32,12,24,1]{2,1,3,0:T(8,128)S(1)} %copy-done.4, f32[32,12,8,768]{3,2,1,0:T(8,128)S(1)} %bitcast.82), kind=kOutput, calls=%fused_computation | convolution fusion | flops 679477248 | bytes 28348416 | tf_op jit(solution)/shard_map/becT,becsd->bsTd/dot_general | solution.py:155
  226.7 0.0 reduce-scatter.2.cloned.1.call-update
  226.7 0.0 copy-start.1
  226.7 0.9 dynamic_slice.43
  227.7 0.1 fusion.53
  227.8 0.8 fusion.31
  228.6 225.2 %all-reduce.4.cloned.1.call-done = bf16[1,6144,16]{1,2,0:T(8,128)(2,1)} async-done(((bf16[1,6144,16]{1,2,0:T(8,128)(2,1)}), bf16[1,6144,16]{1,2,0:T(8,128)(2,1)}) %all-reduce.4.cloned.1.call-update) | async-done | bytes 196624 | tf_op jit(solution)/shard_map/psum | solution.py:192
  453.8 1.7 convert_element_type.125
  455.5 1286.4 %reduce-scatter.2.cloned.1.call-done = f32[1,24,768]{2,1,0:T(8,128)} async-done(((f32[256,24,768]{2,1,0:T(8,128)}), f32[1,24,768]{2,1,0:T(8,128)}) %reduce-scatter.2.cloned.1.call-update) | async-done | bytes 73744 | tf_op jit(solution)/shard_map/reduce_scatter | solution.py:159
  1741.9 1.0 fusion.42
  1742.9 13.0 psum.42
  1755.9 1.0 fusion.44
  1756.9 0.0 copy-start.7
  1756.9 0.1 fusion.52
  1757.0 25.2 %all-reduce = (bf16[24,16]{0,1:T(8,128)(2,1)S(1)}, bf16[24,16]{0,1:T(8,128)(2,1)S(1)}) all-reduce(f32[24,16]{0,1:T(8,128)S(1)} %fusion.52, f32[24,16]{0,1:T(8,128)S(1)} %fusion.53), channel_id=1, replica_groups=mesh['dp'=32,'shard'=8] {'shard'}, use_global_device_ids=true, to_apply=%region_10.11 | all-reduce | flops 768 | bytes 4608 | tf_op jit(solution)/shard_map/psum | solution.py:184
  1782.2 0.1 fusion.30
  1782.3 0.1 fusion.29
  1782.5 158.9 %all-reduce.1 = (bf16[768,16]{0,1:T(8,128)(2,1)S(1)}, bf16[16,768]{1,0:T(8,128)(2,1)S(1)}) all-reduce(bf16[768,16]{0,1:T(8,128)(2,1)S(1)} %fusion.30, bf16[16,768]{1,0:T(8,128)(2,1)S(1)} %fusion.29), channel_id=1, replica_groups=mesh['dp'=32,'shard'=8] {'dp'}, use_global_device_ids=true, to_apply=%region_11.12 | all-reduce | flops 24576 | bytes 98304 | tf_op jit(solution)/shard_map/psum | solution.py:193
  1941.3 0.6 convert_element_type.129
  1942.0 0.6 convert_element_type.132
  (32 shorter events, 0.1 us)
Async XLA Ops:
  7.2 162.3 %copy-start = (bf16[1,6144,256]{2,1,0:T(8,128)(2,1)S(1)}, bf16[1,6144,256]{2,1,0:T(8,128)(2,1)}, u32[]{:S(2)}) copy-start(bf16[1,6144,256]{2,1,0:T(8,128)(2,1)} %param.20) | copy-start | bytes 9437188
  7.2 79.9 %all-gather.8.cloned.1.call-start = ((), (), s32[]{:S(2)}) async-start(), calls=%async_computation.4 | async-start | bytes 6488064 | tf_op jit(solution)/shard_map/all_gather | solution.py:113
  8.5 0.5 copy-start.12
  13.7 143.0 %all-gather.6.cloned.1.call-start = ((), (), s32[]{:S(2)}) async-start(), calls=%async_computation.3 | async-start | bytes 6488064 | tf_op jit(solution)/shard_map/all_gather | solution.py:114
  15.8 438.0 %all-reduce.4.cloned.1.call-start = ((), (), s32[]{:S(2)}) async-start(), calls=%async_computation.2 | async-start | bytes 393216 | tf_op jit(solution)/shard_map/psum | solution.py:192
  67.1 27.6 %copy-start.5 = (bf16[1,6144,16]{1,2,0:T(8,128)(2,1)S(1)}, bf16[1,6144,16]{1,2,0:T(8,128)(2,1)}, u32[]{:S(2)}) copy-start(bf16[1,6144,16]{1,2,0:T(8,128)(2,1)} %param.22) | copy-start | bytes 589828
  94.7 3.8 copy-start.2
  164.4 4.8 copy-start.6
  164.4 4.8 copy-start.9
  169.5 14.3 slice-start
  173.4 5.2 copy-start.3
  173.4 10.4 slice-start.1
  186.4 1555.5 %reduce-scatter.2.cloned.1.call-start = ((), (), s32[]{:S(2)}) async-start(), calls=%async_computation.1 | async-start | bytes 18948096 | tf_op jit(solution)/shard_map/reduce_scatter | solution.py:159
  197.5 8.0 copy-start.4
  226.7 1.0 copy-start.8
  226.7 1.0 copy-start.10
  226.7 1529.2 %copy-start.13 = (f32[24]{0:T(128)S(1)}, f32[24]{0:T(128)}, u32[]{:S(2)}) copy-start(f32[24]{0:T(128)} %copy-done.12) | copy-start | bytes 292
  226.7 1530.2 %copy-start.11 = (bf16[16,768]{1,0:T(8,128)(2,1)S(1)}, bf16[16,768]{1,0:T(8,128)(2,1)}, u32[]{:S(2)}) copy-start(bf16[16,768]{1,0:T(8,128)(2,1)} %param.25) | copy-start | bytes 73732
  226.7 1715.9 %copy-start.1 = (bf16[1,6144,256]{2,1,0:T(8,128)(2,1)S(1)}, bf16[1,6144,256]{2,1,0:T(8,128)(2,1)}, u32[]{:S(2)}) copy-start(bf16[1,6144,256]{2,1,0:T(8,128)(2,1)} %param.20) | copy-start | bytes 9437188
  1756.9 185.7 %copy-start.7 = (bf16[24,768]{1,0:T(8,128)(2,1)}, bf16[24,768]{1,0:T(8,128)(2,1)S(1)}, u32[]{:S(2)}) copy-start(bf16[24,768]{1,0:T(8,128)(2,1)S(1)} %fusion.44) | copy-start | bytes 110596
Sparse Core Ops, SparseCore 0:
  13.9 73.2 all-gather.7
  89.7 67.0 all-gather.5
  186.5 267.2 all-reduce.3
  456.3 1285.5 reduce-scatter.1
where the time goes:
time: 1950 us
  waiting for transfers between devices  1590 us (82%)
  blocking collectives  246 us (13%)
  matrix products  67.2 us (3%)
  local copies, waits for them, and re-layouts  26.9 us (1%)
    reduce_scatter x1, waiting for transfers between devices, body(): lax.psum_scatter(token_term, ('dp', 'shard'), scatter_dimension=0, tiled=...  1290 us
    psum x1, waiting for transfers between devices, body(): lax.psum(grads_a.astype(jnp.bfloat16), 'dp').astype(jnp.float32)  225 us
    psum x1, blocking collectives, body(): lax.psum(first_factor_partial.astype(jnp.bfloat16), 'dp')  159 us
    all_gather x1, waiting for transfers between devices, body(): lax.all_gather(packed_output_gradient, 'dp', axis=0, tiled=True)  54.1 us
    all_gather x1, blocking collectives, body(): all_routes = lax.all_gather(routes, 'dp', axis=0, tiled=True)  49.1 us
  transfers between devices with their start and end apart: 4, of which 4 were waited for; matrix products, arithmetic and copies ran while one was open for 3% of the time, Pallas kernels for 0%

commit v1 on v0

v1 whole, which is shorter than its diff:
```python
import functools

import jax
import jax.numpy as jnp
from jax import lax
from jax.experimental import pallas as pl
from jax.experimental.pallas import tpu as pltpu
from jax.sharding import PartitionSpec as P

CAP = 12
EPSILON = 1e-05
SCALE = 0.5
NX = 4
F32 = jnp.float32
BF16 = jnp.bfloat16
MESH = pl.DeviceIdType.MESH
NN = (((1,), (0,)), ((), ()))
NT = (((1,), (1,)), ((), ()))


def mm(a, b, dims=NN):
    return lax.dot_general(a, b, dims, preferred_element_type=F32)


def two_parts(value):
    high = value.astype(BF16)
    return high, (value - high.astype(F32)).astype(BF16)


def column(row, count):
    eye = lax.broadcasted_iota(jnp.int32, (count, count), 0) == lax.broadcasted_iota(
        jnp.int32, (count, count), 1
    )
    return jnp.sum(jnp.where(eye, jnp.broadcast_to(row, (count, count)), 0.0), axis=1, keepdims=True)


def row_of(col, count):
    eye = lax.broadcasted_iota(jnp.int32, (count, count), 0) == lax.broadcasted_iota(
        jnp.int32, (count, count), 1
    )
    return jnp.sum(jnp.where(eye, jnp.broadcast_to(col, (count, count)), 0.0), axis=0, keepdims=True)


def kernel(
    nz,
    ns,
    kc,
    hid_ref,
    mix_ref,
    og_ref,
    gain_ref,
    routes_ref,
    rw_ref,
    wg_hbm,
    wu_hbm,
    wd_hbm,
    a1_hbm,
    a2_ref,
    att1_ref,
    att2_ref,
    rg_ref,
    ga_ref,
    gs_ref,
    af_ref,
    as_ref,
    wg,
    wu,
    wd,
    a1,
    rb,
    sb0,
    G,
    acc_g,
    acc_u,
    acc_d,
    acc_l,
    dg,
    du,
    bk,
    TB,
    TR,
    SB,
    XR1,
    XR2,
    ZB,
    ZR,
    EB,
    E,
    PB,
    PR,
    A,
    AR,
    F,
    rad_ref,
    w_sem,
    p0_s,
    p0_r,
    z_s,
    z_r,
    x_s,
    x_r,
    c_s,
    c_r,
    t_s,
    t_r,
    x1_s,
    x1_r,
    x2_s,
    x2_r,
    zz_s,
    zz_r,
    e_s,
    e_r,
    e_l,
    q_s,
    q_r,
    a_s,
    a_r,
    f_s,
    f_r,
):
    nch = ns // 2
    nd = NX * nz * 2
    chips = NX * nz
    toks = hid_ref.shape[0]
    width = hid_ref.shape[1]
    hw = width // 2
    frame = chips * 32
    rows = chips * 24
    lanes = kc // 128
    d = lax.axis_index("dp")
    s = lax.axis_index("shard")
    core = lax.rem(d, 2)
    zh = lax.rem(d // 2, nz)
    xx = d // (2 * nz)
    q = xx * nz + zh
    other = 1 - core

    def dp_of(x_, z_, c_):
        return (x_ * nz + z_) * 2 + c_

    xp, xm, x2 = lax.rem(xx + 1, NX), lax.rem(xx + 3, NX), lax.rem(xx + 2, NX)
    dev_c = (dp_of(xx, zh, other), s)
    dev_xp = (dp_of(xp, zh, core), s)
    dev_xm = (dp_of(xm, zh, core), s)

    def zpeer(o):
        return lax.rem(zh + o, nz)

    def dev_z(o):
        return (dp_of(xx, zpeer(o), core), s)

    def rcopy(src, dst, ssem, rsem, dev):
        return pltpu.make_async_remote_copy(
            src_ref=src, dst_ref=dst, send_sem=ssem, recv_sem=rsem, device_id=dev, device_id_type=MESH
        )

    w_copies = [
        pltpu.make_async_copy(a1_hbm, a1, w_sem.at[0]),
        pltpu.make_async_copy(wg_hbm, wg, w_sem.at[1]),
        pltpu.make_async_copy(wu_hbm, wu, w_sem.at[2]),
    ] + [
        pltpu.make_async_copy(wd_hbm.at[:, pl.ds(i * kc, kc)], wd.at[i], w_sem.at[3 + i])
        for i in range(2 * nch)
    ]
    for copy in w_copies:
        copy.start()

    barrier = pltpu.get_barrier_semaphore()

    def greet_dp(o, carry):
        pl.semaphore_signal(barrier, inc=1, device_id=(lax.rem(d + o, nd), s), device_id_type=MESH)
        return carry

    lax.fori_loop(1, nd, greet_dp, 0)

    def greet_shard(o, carry):
        there = lax.rem(s + o, ns)
        pl.semaphore_signal(barrier, inc=1, device_id=(d, there), device_id_type=MESH)
        pl.semaphore_signal(barrier, inc=1, device_id=(dp_of(xx, zh, other), there), device_id_type=MESH)
        return carry

    lax.fori_loop(1, ns, greet_shard, 0)

    hid = hid_ref[...].astype(F32)
    radius = lax.rsqrt(jnp.mean(hid * hid, axis=1, keepdims=True) + EPSILON)
    rad_ref[...] = jnp.broadcast_to(radius, rad_ref.shape)
    normed = hid * radius * gain_ref[...]
    tok = jnp.concatenate([normed, og_ref[...].astype(F32)], axis=0).astype(BF16)

    r0 = column(routes_ref[0:1, :].astype(F32), toks)
    r1 = column(routes_ref[1:2, :].astype(F32), toks)
    w0 = column(rw_ref[0:1, :], toks)
    w1 = column(rw_ref[1:2, :], toks)
    lane = lax.broadcasted_iota(jnp.int32, (toks, 128), 1)
    lower = (
        lax.broadcasted_iota(jnp.int32, (toks, toks), 0) > lax.broadcasted_iota(jnp.int32, (toks, toks), 1)
    ).astype(F32).astype(BF16)
    lane_e = (lane // 16).astype(F32)
    named_all = jnp.where((r0 == lane_e) | (r1 == lane_e), 1.0, 0.0)
    slot_all = mm(lower, named_all.astype(BF16))
    place_f = lax.rem(lane, 16).astype(F32)
    choose_all = jnp.where(slot_all + (4 * core).astype(F32) == place_f, named_all, 0.0).astype(BF16)
    mine = jnp.broadcast_to(s.astype(F32), (toks, 128))
    hit0 = jnp.where(r0 == mine, 1.0, 0.0)
    hit1 = jnp.where(r1 == mine, 1.0, 0.0)
    named = hit0 + hit1
    weight = hit0 * w0 + hit1 * w1
    slot = mm(lower, named.astype(BF16)) + (CAP * core).astype(F32)
    row_x = jnp.where(lane < 24, lane, -1).astype(F32)
    row_y = jnp.where(
        (lane >= 24) & (lane < 32), lane - 8, jnp.where((lane >= 32) & (lane < 48), lane - 32, -1)
    ).astype(F32)
    hot_x = jnp.where(slot == row_x, named, 0.0)
    hot_y = jnp.where(slot == row_y, named, 0.0)
    blank = jnp.zeros((128 - 2 * toks, 128), F32)
    hot = jnp.concatenate([hot_x, hot_y, blank], axis=0).T
    scale = jnp.concatenate([hot_x, hot_y * weight, blank], axis=0).T
    hot = hot[0:48, 0:48].astype(BF16)
    scale = jnp.sum(scale[0:48, :], axis=1, keepdims=True)
    for j in range(2 * nch):
        part = mm(hot, tok[:, j * kc : (j + 1) * kc]) * scale
        sb0[j] = part.astype(BF16)

    pl.semaphore_wait(barrier, nd - 1 + 2 * (ns - 1))

    swap = rcopy(sb0.at[pl.ds(other * nch, nch)], rb, p0_s, p0_r, dev_c)
    swap.start()

    PB[40:64, 0:16] = mm(mix_ref[...], att1_ref[...], NT)

    acc_g[...] = jnp.zeros_like(acc_g)
    acc_u[...] = jnp.zeros_like(acc_u)
    acc_d[...] = jnp.zeros_like(acc_d)
    acc_l[...] = jnp.zeros_like(acc_l)

    swap.wait_recv()

    def z_copy(k, o):
        ref = G.at[core * nch + k, q]
        return rcopy(ref, ref, z_s.at[k, o - 1], z_r.at[k, o - 1], dev_z(o))

    def z_start(k, carry):
        G[core * nch + k, q] = (sb0[core * nch + k].astype(F32) + rb[k].astype(F32)).astype(BF16)
        for o in range(1, nz):
            z_copy(k, o).start()
        return carry

    lax.fori_loop(0, nch, z_start, 0)

    def x_copy(k, which):
        ch = core * nch + k
        half = nz // 2
        if which == 0:
            ref, dev = G.at[ch, pl.ds(xx * nz, nz)], dev_xp
        elif which == 1:
            ref, dev = G.at[ch, pl.ds(xx * nz, nz)], dev_xm
        elif which == 2:
            ref, dev = G.at[ch, pl.ds(xm * nz, half)], dev_xp
        else:
            ref, dev = G.at[ch, pl.ds(xp * nz + half, half)], dev_xm
        return rcopy(ref, ref, x_s.at[k, which], x_r.at[k, which], dev)

    def c_copy(k):
        ref = G.at[core * nch + k]
        return rcopy(ref, ref, c_s.at[k], c_r.at[k], dev_c)

    def product(ch):
        xrows = G[ch, :, 0:32, :].reshape(frame, kc)
        yrows = G[ch, :, 16:48, :].reshape(frame, kc)
        at = pl.ds(pl.multiple_of(ch * kc, kc), kc)
        acc_g[...] += mm(xrows, wg[at, :])
        acc_u[...] += mm(xrows, wu[at, :])
        acc_l[:, 0:16] += mm(xrows, a1[ch], NT)
        acc_d[...] += mm(yrows, wd[ch], NT)

    def gather_step(i, carry):
        @pl.when(i < nch)
        def _():
            for o in range(1, nz):
                z_copy(i, o).wait_recv()
            x_copy(i, 0).start()
            x_copy(i, 1).start()

        @pl.when((i >= 1) & (i < nch + 1))
        def _():
            k = i - 1
            x_copy(k, 0).wait_recv()
            x_copy(k, 2).start()
            x_copy(k, 1).wait_recv()
            x_copy(k, 3).start()

        @pl.when(i == 2)
        def _():
            for copy in w_copies:
                copy.wait()

        @pl.when((i >= 2) & (i < nch + 2))
        def _():
            k = i - 2
            x_copy(k, 2).wait_recv()
            x_copy(k, 3).wait_recv()
            c_copy(k).start()
            product(core * nch + k)

        @pl.when(i >= 3)
        def _():
            k = i - 3
            c_copy(k).wait_recv()
            product(other * nch + k)

        return carry

    lax.fori_loop(0, nch + 3, gather_step, 0)

    low = acc_l[...].astype(BF16)
    gate = acc_g[...] + SCALE * mm(low[:, 0:16], a2_ref[...])
    hidden = gate.shape[1]
    gate = gate.reshape(chips, 32, hidden)[:, 0:24, :]
    upper = acc_u[...].reshape(chips, 32, hidden)[:, 0:24, :]
    dact = acc_d[...].reshape(chips, 32, hidden)
    dact = jnp.concatenate([dact[:, 16:32, :], dact[:, 8:16, :]], axis=1)
    sig = 1.0 / (1.0 + jnp.exp(-gate))
    dgate = dact * upper * sig * (1.0 + gate * (1.0 - sig))
    dup = dact * gate * sig
    du[...] = dup.reshape(rows, hidden).astype(BF16)
    dgate_rows = dgate.reshape(rows, hidden).astype(BF16)
    dg[...] = dgate_rows
    bk[...] = (SCALE * mm(dgate_rows, a2_ref[...], NT)).astype(BF16)
    dgate_frame = (
        jnp.concatenate([dgate, jnp.zeros((chips, 8, hidden), F32)], axis=1)
        .reshape(frame, hidden)
        .astype(BF16)
    )
    low_t = acc_l[...].T[0:16, :].astype(BF16)
    gs_ref[...] = SCALE * mm(low_t, dgate_frame)
    back_t = SCALE * mm(a2_ref[...], dgate_frame, NT)
    n_att = 4 * lanes
    f_lanes = frame // 128
    for j in range(2 * f_lanes):
        r, l = j // f_lanes, j % f_lanes
        A[n_att + j] = back_t[r * 8 : r * 8 + 8, l * 128 : (l + 1) * 128]

    slab = nz * 24
    half_slab = slab // 2

    def term(ch):
        at = pl.ds(pl.multiple_of(ch * kc, kc), kc)
        return mm(dg[...], wg[at, :], NT) + mm(du[...], wu[at, :], NT) + mm(bk[...], a1[ch])

    def t_copy(k):
        return rcopy(TB.at[k], TR.at[k], t_s.at[k], t_r.at[k], dev_c)

    def x1_copy(k, which):
        if which == 0:
            return rcopy(
                SB.at[k, x2, pl.ds(0, half_slab)], XR1.at[k, 0], x1_s.at[k, 0], x1_r.at[k, 0], dev_xp
            )
        return rcopy(
            SB.at[k, x2, pl.ds(half_slab, half_slab)], XR1.at[k, 1], x1_s.at[k, 1], x1_r.at[k, 1], dev_xm
        )

    def x2_copy(k, which):
        if which == 0:
            return rcopy(SB.at[k, xp], XR2.at[k, 0], x2_s.at[k, 0], x2_r.at[k, 0], dev_xp)
        return rcopy(SB.at[k, xm], XR2.at[k, 1], x2_s.at[k, 1], x2_r.at[k, 1], dev_xm)

    def zz_copy(k, o):
        return rcopy(ZB.at[k, zpeer(o)], ZR.at[k, o - 1], zz_s.at[k, o - 1], zz_r.at[k, o - 1], dev_z(o))

    def e_copy(k, c_):
        return rcopy(EB.at[k, c_], E.at[s], e_s.at[k, c_], e_r.at[s], (dp_of(xx, zh, c_), core * nch + k))

    def e_local(k, c_):
        return pltpu.make_async_copy(EB.at[k, c_], E.at[s], e_l)

    def e_self(k, c_):
        return (core * nch + k == s) & (core == c_)

    def reduce_step(i, carry):
        @pl.when(i < nch)
        def _():
            k = i
            TB[k] = term(other * nch + k).astype(BF16)
            t_copy(k).start()
            own = term(core * nch + k)
            t_copy(k).wait_recv()
            total = own + TR[k].astype(F32)
            SB[k] = total.astype(BF16).reshape(NX, slab, kc)
            x1_copy(k, 0).start()
            x1_copy(k, 1).start()

        @pl.when((i >= 1) & (i < nch + 1))
        def _():
            k = i - 1
            for which, there, at in ((0, xp, 0), (1, xm, half_slab)):
                x1_copy(k, which).wait_recv()
                SB[k, there, at : at + half_slab] = (
                    SB[k, there, at : at + half_slab].astype(F32) + XR1[k, which].astype(F32)
                ).astype(BF16)
                x2_copy(k, which).start()

        @pl.when((i >= 2) & (i < nch + 2))
        def _():
            k = i - 2
            x2_copy(k, 0).wait_recv()
            x2_copy(k, 1).wait_recv()
            total = SB[k, xx].astype(F32) + XR2[k, 0].astype(F32) + XR2[k, 1].astype(F32)
            for z_ in range(nz):
                piece = total[z_ * 24 : z_ * 24 + 24]
                ZB[k, z_] = jnp.concatenate([piece[:, : kc // 2], piece[:, kc // 2 :]], axis=0).astype(BF16)
            for o in range(1, nz):
                zz_copy(k, o).start()

        @pl.when(i >= 3)
        def _():
            k = i - 3
            total = ZB[k, zh].astype(F32)
            for o in range(1, nz):
                zz_copy(k, o).wait_recv()
                total = total + ZR[k, o - 1].astype(F32)
            total = jnp.concatenate([total[0:24], total[24:48]], axis=1)
            EB[k, 0] = total[0:16].astype(BF16)
            EB[k, 1] = total[8:24].astype(BF16)
            for c_ in range(2):
                self_ = e_self(k, c_)

                @pl.when(self_)
                def _():
                    e_local(k, c_).start()
                    e_local(k, c_).wait()

                @pl.when(jnp.logical_not(self_))
                def _():
                    e_copy(k, c_).start()

        return carry

    lax.fori_loop(0, nch + 3, reduce_step, 0)

    def e_wait(o, carry):
        there = lax.rem(s + o, ns)
        rcopy(E.at[there], E.at[there], e_s.at[0, 0], e_r.at[there], dev_c).wait_recv()
        return carry

    lax.fori_loop(1, ns, e_wait, 0)
    home = s // nch == core

    @pl.when(jnp.logical_not(home))
    def _():
        rcopy(E.at[s], E.at[s], e_s.at[0, 0], e_r.at[s], dev_c).wait_recv()

    at = pl.ds(pl.multiple_of(s * kc, kc), kc)
    grad = mm(choose_all[:, 0 : 16 * ns], E[...].reshape(16 * ns, kc))
    spread = gain_ref[:, at] * grad
    hid_cols = hid_ref[:, at]
    hid_f = hid_cols.astype(F32)
    rad = rad_ref[:, 0:1]
    base = og_ref[:, at].astype(F32) + rad * spread
    stat_part = jnp.sum(spread * hid_f, axis=1, keepdims=True)
    PB[0:8, 0:toks] = jnp.broadcast_to(row_of(stat_part, toks), (8, toks))
    high, rest = two_parts(base)
    PB[8:24, 0:toks] = mm(att2_ref[...], high, NT) + mm(att2_ref[...], rest, NT)
    PB[24:40, 0:toks] = mm(att2_ref[...], hid_cols, NT)

    def q_copy(o):
        return rcopy(PB, PR.at[o - 1], q_s.at[o - 1], q_r.at[o - 1], (d, lax.rem(s + o, ns)))

    for o in range(1, ns):
        q_copy(o).start()
    total = PB[...]
    for o in range(1, ns):
        q_copy(o).wait_recv()
        total = total + PR[o - 1]
    stat_row = total[0:1, 0:toks] / width
    factor = rad * rad * rad * column(stat_row, toks)
    rg = (base - hid_f * factor).astype(BF16)
    rg_ref[...] = rg
    factor_row = row_of(factor, toks)
    back_low = (total[8:24, 0:toks] - total[24:40, 0:toks] * factor_row).astype(BF16)
    mixed_t = jnp.concatenate([total[40:64, :], jnp.zeros((104, 128), F32)], axis=0).T
    mixed_low = mixed_t[0:16, 0:toks].astype(BF16)
    first = SCALE * mm(back_low, mix_ref[...])
    second = SCALE * mm(mixed_low, rg)
    for j in range(lanes):
        cols = slice(j * 128, (j + 1) * 128)
        A[j] = first[0:8, cols]
        A[lanes + j] = first[8:16, cols]
        A[2 * lanes + j] = second[0:8, cols]
        A[3 * lanes + j] = second[8:16, cols]

    def a_copy(o):
        to = lax.rem(d + o, nd)
        return rcopy(A.at[to], AR.at[o - 1], a_s.at[o - 1], a_r.at[o - 1], (to, s))

    def f_copy(o):
        to = lax.rem(d + o, nd)
        return rcopy(F.at[d], F.at[d], f_s.at[o - 1], f_r.at[d], (to, s))

    def a_start(o, carry):
        a_copy(o).start()
        return carry

    lax.fori_loop(1, nd, a_start, 0)

    def a_add(o, tile):
        a_copy(o).wait_recv()
        return tile + AR[o - 1]

    F[d] = lax.fori_loop(1, nd, a_add, A[d])

    def f_start(o, carry):
        f_copy(o).start()
        return carry

    lax.fori_loop(1, nd, f_start, 0)

    def f_wait(o, carry):
        frm = lax.rem(d + o, nd)
        rcopy(F.at[frm], F.at[frm], f_s.at[0], f_r.at[frm], dev_c).wait_recv()
        return carry

    lax.fori_loop(1, nd, f_wait, 0)

    for j in range(lanes):
        cols = slice(j * 128, (j + 1) * 128)
        af_ref[0:8, cols] = F[j]
        af_ref[8:16, cols] = F[lanes + j]
        as_ref[0:8, cols] = F[2 * lanes + j]
        as_ref[8:16, cols] = F[3 * lanes + j]
    back_full = jnp.concatenate(
        [
            jnp.concatenate([F[n_att + r * f_lanes + l] for l in range(f_lanes)], axis=1)
            for r in range(2)
        ],
        axis=0,
    )
    high, rest = two_parts(back_full)
    both = jnp.concatenate([high, rest], axis=0)

    def first_gradient(ch, carry):
        xrows = G[ch, :, 0:32, :].reshape(frame, kc)
        pair = mm(both, xrows)
        ga_ref[:, pl.ds(pl.multiple_of(ch * kc, kc), kc)] = pair[0:16] + pair[16:32]
        return carry

    lax.fori_loop(0, 2 * nch, first_gradient, 0)

    swap.wait_send()

    def drain(k, carry):
        for o in range(1, nz):
            z_copy(k, o).wait_send()
            zz_copy(k, o).wait_send()
        for which in range(4):
            x_copy(k, which).wait_send()
        c_copy(k).wait_send()
        t_copy(k).wait_send()
        for which in range(2):
            x1_copy(k, which).wait_send()
            x2_copy(k, which).wait_send()
        for c_ in range(2):

            @pl.when(jnp.logical_not(e_self(k, c_)))
            def _():
                e_copy(k, c_).wait_send()

        return carry

    lax.fori_loop(0, nch, drain, 0)
    for o in range(1, ns):
        q_copy(o).wait_send()

    def drain_dp(o, carry):
        a_copy(o).wait_send()
        f_copy(o).wait_send()
        return carry

    lax.fori_loop(1, nd, drain_dp, 0)


def fused(nz, ns, *args):
    hid, mix = args[0], args[1]
    width, kc = hid.shape[1], mix.shape[1]
    toks = hid.shape[0]
    hidden = args[6].shape[1]
    nch = ns // 2
    nd = NX * nz * 2
    chips = NX * nz
    rows, frame = chips * 24, chips * 32
    slab = nz * 24
    zo = max(nz - 1, 1)
    vm = pltpu.VMEM
    dma = pltpu.SemaphoreType.DMA
    scratch = [
        vm((width, hidden), BF16),
        vm((width, hidden), BF16),
        vm((2 * nch, hidden, kc), BF16),
        vm((2 * nch, 16, kc), BF16),
        vm((nch, 48, kc), BF16),
        vm((2 * nch, 48, kc), BF16),
        vm((2 * nch, chips, 48, kc), BF16),
        vm((frame, hidden), F32),
        vm((frame, hidden), F32),
        vm((frame, hidden), F32),
        vm((frame, 128), F32),
        vm((rows, hidden), BF16),
        vm((rows, hidden), BF16),
        vm((rows, 16), BF16),
        vm((nch, rows, kc), BF16),
        vm((nch, rows, kc), BF16),
        vm((nch, NX, slab, kc), BF16),
        vm((nch, 2, slab // 2, kc), BF16),
        vm((nch, 2, slab, kc), BF16),
        vm((nch, nz, 48, kc // 2), BF16),
        vm((nch, zo, 48, kc // 2), BF16),
        vm((nch, 2, 16, kc), BF16),
        vm((ns, 16, kc), BF16),
        vm((64, 128), F32),
        vm((ns - 1, 64, 128), F32),
        vm((nd, 8, 128), F32),
        vm((nd - 1, 8, 128), F32),
        vm((nd, 8, 128), F32),
        vm((toks, 128), F32),
        dma((3 + 2 * nch,)),
        dma,
        dma,
        dma((nch, zo)),
        dma((nch, zo)),
        dma((nch, 4)),
        dma((nch, 4)),
        dma((nch,)),
        dma((nch,)),
        dma((nch,)),
        dma((nch,)),
        dma((nch, 2)),
        dma((nch, 2)),
        dma((nch, 2)),
        dma((nch, 2)),
        dma((nch, zo)),
        dma((nch, zo)),
        dma((nch, 2)),
        dma((ns,)),
        dma,
        dma((ns - 1,)),
        dma((ns - 1,)),
        dma((nd - 1,)),
        dma((nd - 1,)),
        dma((nd - 1,)),
        dma((nd,)),
    ]
    vmem = pl.BlockSpec(memory_space=pltpu.VMEM)
    hbm = pl.BlockSpec(memory_space=pl.ANY)
    return pl.pallas_call(
        functools.partial(kernel, nz, ns, kc),
        out_shape=(
            jax.ShapeDtypeStruct((toks, kc), BF16),
            jax.ShapeDtypeStruct((16, width), F32),
            jax.ShapeDtypeStruct((16, hidden), F32),
            jax.ShapeDtypeStruct((16, kc), F32),
            jax.ShapeDtypeStruct((16, kc), F32),
        ),
        in_specs=[vmem] * 6 + [hbm] * 4 + [vmem] * 3,
        out_specs=(vmem,) * 5,
        scratch_shapes=scratch,
        compiler_params=pltpu.CompilerParams(
            collective_id=0, has_side_effects=True, vmem_limit_bytes=58 * 1024 * 1024
        ),
        cost_estimate=pl.CostEstimate(
            flops=2 * rows * width * hidden * 5, bytes_accessed=6 * width * hidden, transcendentals=0
        ),
    )(*args)


def body(nz, hid, mix, og, gain, routes, rw, wg, wu, wd, a1, a2, att1, att2):
    ns = lax.axis_size("shard")
    width, kc = hid.shape[1], mix.shape[1]
    a1_chunks = a1[0].T.reshape(16, ns, kc).swapaxes(0, 1)
    rg, ga, gs, af, sec = fused(
        nz,
        ns,
        hid,
        mix,
        og,
        gain.reshape(1, width),
        routes.T,
        rw.T,
        wg[0],
        wu[0],
        wd[0],
        a1_chunks,
        a2[0],
        att1.T,
        att2,
    )
    return rg, ga.T[None], gs[None], af.T, sec


def solution(mesh):
    nz = mesh.shape["dp"] // (2 * NX)
    in_specs = (
        P("dp", None),
        P("dp", "shard"),
        P("dp", None),
        P(),
        P("dp", None),
        P("dp", None),
        P("shard", None, "dp"),
        P("shard", None, "dp"),
        P("shard", "dp", None),
        P("shard", None, None),
        P("shard", None, "dp"),
        P("shard", None),
        P(None, "shard"),
    )
    out_specs = (
        P("dp", "shard"),
        P("shard", None, None),
        P("shard", None, "dp"),
        P("shard", None),
        P(None, "shard"),
    )
    return jax.shard_map(
        functools.partial(body, nz), mesh=mesh, in_specs=in_specs, out_specs=out_specs, check_vma=False
    )
```

time: 1950 us -> 142 us (0.07)
  waiting for transfers between devices: 1590 us -> 0 us
  blocking collectives: 246 us -> 0 us
  Pallas kernels: 0 us -> 133 us
  matrix products: 67.2 us -> 0 us
    reduce_scatter x1 -> x0, waiting for transfers between devices: 1290 us -> none  [body(): lax.psum_scatter(token_term, ('dp', 'shard'), scatter_dimension=0, tiled=...]
    psum x1 -> x0, waiting for transfers between devices: 225 us -> none  [body(): lax.psum(grads_a.astype(jnp.bfloat16), 'dp').astype(jnp.float32)]
    psum x3 -> x0, blocking collectives: 197 us -> none  [the longest x1 159 us: body(): lax.psum(first_factor_partial.astype(jnp.bfloat16), 'dp')]
    pallas_call x0 -> x1, Pallas kernels: none -> 133 us  [fused(): pl.pallas_call(functools.partial(kernel, nz, ns, kc), out_shape=(jax.Shap...]
    all_gather x2 -> x0, waiting for transfers between devices: 74.1 us -> none  [the longest x1 54.1 us: body(): lax.all_gather(packed_output_gradient, 'dp', axis=0, tiled=True)]
    dot_general x18 -> x0, matrix products: 67.2 us -> none  [the longest x1 21.2 us: body(): jnp.einsum('becT,becsd->bsTd', every_choose, row_terms, precision=lax.Pre...]
    all_gather x1 -> x0, blocking collectives: 49.1 us -> none  [body(): all_routes = lax.all_gather(routes, 'dp', axis=0, tiled=True)]
  transfers between devices with their start and end apart: 4 -> 0, of which waited for: 4 -> 0; matrix products, arithmetic and copies ran while one was open for 3% -> 0% of each run, Pallas kernels for 0% -> 0%
where the time goes in v1:
time: 142 us
  Pallas kernels  133 us (94%)
  local copies, waits for them, and re-layouts  8.93 us (6%)
    pallas_call x1, Pallas kernels, fused(): pl.pallas_call(functools.partial(kernel, nz, ns, kc), out_shape=(jax.Shap...  133 us
    unnamed x5, local copies, waits for them, and re-layouts  7.32 us

profile of v1, /device:TPU:1, one launch (start us, length us, event | category | flops | bytes accessed | tf_op | source)
XLA Modules:
  0.0 142.1 jit_solution(9532127096286120415)
XLA Ops:
  0.6 1.6 %copy.21 = bf16[2,8,8,768]{3,2,0,1:T(8,128)(2,1)} copy(bf16[2,8,8,768]{3,2,1,0:T(8,128)(2,1)} %bitcast.24) | data formatting | bytes 393216 | tf_op jit(solution)/shard_map/reshape | solution.py:678
  2.2 132.5 %shard_map.164 = (bf16[24,768]{1,0:T(8,128)(2,1)}, f32[16,6144]{1,0:T(8,128)}, f32[16,256]{1,0:T(8,128)}, f32[16,768]{1,0:T(8,128)}, f32[16,768]{1,0:T(8,128)}) custom-call(bf16[24,6144]{1,0:T(8,128)(2,1)} %hid_ref.1, bf16[24,768]{1,0:T(8,128)(2,1)} %mix_ref.1, bf16[24,6144]{1,0:T(8,128)(2,1)} %og_ref.1, f32[1,6144]{1,0:T(1,128)} %bitcast.31, ...), custom_call_target="tpu_custom_call" | custom-call | flops 6039797760 | bytes 9437184 | tf_op jit(solution)/shard_map/pallas_call | solution.py:654
  134.8 1.4 copy.27
  136.2 1.8 %copy.28 = f32[1,6144,16]{1,2,0:T(8,128)} copy(f32[1,6144,16]{1,2,0:T(8,128)} %bitcast.23) | data formatting | bytes 786432
  137.9 1.3 copy.29
  139.3 1.4 copy.30
  140.7 1.4 copy.31

commit v2 on v1

v2 whole, which is shorter than its diff:
```python
import functools

import jax
import jax.numpy as jnp
from jax import lax
from jax.experimental import pallas as pl
from jax.experimental.pallas import tpu as pltpu
from jax.sharding import PartitionSpec as P

CAP = 12
EPSILON = 1e-05
SCALE = 0.5
NX = 4
F32 = jnp.float32
BF16 = jnp.bfloat16
MESH = pl.DeviceIdType.MESH
NN = (((1,), (0,)), ((), ()))
NT = (((1,), (1,)), ((), ()))


def mm(a, b, dims=NN):
    return lax.dot_general(a, b, dims, preferred_element_type=F32)


def two_parts(value):
    high = value.astype(BF16)
    return high, (value - high.astype(F32)).astype(BF16)


def column(row, count):
    eye = lax.broadcasted_iota(jnp.int32, (count, count), 0) == lax.broadcasted_iota(
        jnp.int32, (count, count), 1
    )
    return jnp.sum(jnp.where(eye, jnp.broadcast_to(row, (count, count)), 0.0), axis=1, keepdims=True)


def row_of(col, count):
    eye = lax.broadcasted_iota(jnp.int32, (count, count), 0) == lax.broadcasted_iota(
        jnp.int32, (count, count), 1
    )
    return jnp.sum(jnp.where(eye, jnp.broadcast_to(col, (count, count)), 0.0), axis=0, keepdims=True)


def kernel(
    nz,
    ns,
    kc,
    hid_ref,
    mix_ref,
    og_ref,
    gain_ref,
    routes_ref,
    rw_ref,
    wg_hbm,
    wu_hbm,
    wd_hbm,
    a1_hbm,
    a2_ref,
    att1_ref,
    att2_ref,
    rg_ref,
    ga_ref,
    gs_ref,
    af_ref,
    as_ref,
    wg,
    wu,
    wd,
    a1,
    rb,
    sb0,
    G,
    acc_g,
    acc_u,
    acc_d,
    acc_l,
    dg,
    du,
    bk,
    TB,
    TR,
    SB,
    XR1,
    XR2,
    ZB,
    ZR,
    EB,
    E,
    PB,
    PR,
    at_bufs,
    bk_bufs,
    rad_ref,
    w_sem,
    p0_s,
    p0_r,
    g_s,
    s1_r,
    s2_r,
    c_s,
    c_r,
    t_s,
    t_r,
    x_s,
    x1_r,
    x2_r,
    zz_s,
    zz_r,
    e_s,
    e_r,
    e_l,
    q_s,
    q_r,
    at_sems,
    bk_sems,
):
    nch = ns // 2
    nd = NX * nz * 2
    chips = NX * nz
    toks = hid_ref.shape[0]
    width = hid_ref.shape[1]
    hw = width // 2
    frame = chips * 32
    rows = chips * 24
    lanes = kc // 128
    d = lax.axis_index("dp")
    s = lax.axis_index("shard")
    core = lax.rem(d, 2)
    zh = lax.rem(d // 2, nz)
    xx = d // (2 * nz)
    q = xx * nz + zh
    other = 1 - core

    def dp_of(x_, z_, c_):
        return (x_ * nz + z_) * 2 + c_

    xp, xm, x2 = lax.rem(xx + 1, NX), lax.rem(xx + 3, NX), lax.rem(xx + 2, NX)
    dev_c = (dp_of(xx, zh, other), s)
    dev_xp = (dp_of(xp, zh, core), s)
    dev_xm = (dp_of(xm, zh, core), s)

    def zpeer(o):
        return lax.rem(zh + o, nz)

    def dev_z(o):
        return (dp_of(xx, zpeer(o), core), s)

    def rcopy(src, dst, ssem, rsem, dev):
        return pltpu.make_async_remote_copy(
            src_ref=src, dst_ref=dst, send_sem=ssem, recv_sem=rsem, device_id=dev, device_id_type=MESH
        )

    w_copies = [
        pltpu.make_async_copy(wg_hbm, wg, w_sem.at[0]),
        pltpu.make_async_copy(wu_hbm, wu, w_sem.at[1]),
    ] + [
        pltpu.make_async_copy(wd_hbm.at[:, pl.ds(i * kc, kc)], wd.at[i], w_sem.at[2 + i])
        for i in range(2 * nch)
    ] + [
        pltpu.make_async_copy(a1_hbm.at[:, pl.ds(i * kc, kc)], a1.at[i], w_sem.at[2 + 2 * nch + i])
        for i in range(2 * nch)
    ]
    for copy in w_copies:
        copy.start()

    barrier = pltpu.get_barrier_semaphore()

    def greet(dev):
        pl.semaphore_signal(barrier, inc=1, device_id=dev, device_id_type=MESH)

    group = [(dc, o) for dc in range(2) for o in range(NX)][1:]

    def dev_g(dc, o):
        return (dp_of(lax.rem(xx + o, NX), zh, other if dc else core), s)

    for dc, o in group:
        greet(dev_g(dc, o))
    for o in range(1, nz):
        greet(dev_z(o))

    def greet_shard(o, carry):
        there = lax.rem(s + o, ns)
        greet((d, there))
        greet((dp_of(xx, zh, other), there))
        return carry

    lax.fori_loop(1, ns, greet_shard, 0)

    hid = hid_ref[...].astype(F32)
    radius = lax.rsqrt(jnp.mean(hid * hid, axis=1, keepdims=True) + EPSILON)
    rad_ref[...] = jnp.broadcast_to(radius, rad_ref.shape)
    normed = hid * radius * gain_ref[...]
    tok = jnp.concatenate([normed, og_ref[...].astype(F32)], axis=0).astype(BF16)

    r0 = column(routes_ref[0:1, :].astype(F32), toks)
    r1 = column(routes_ref[1:2, :].astype(F32), toks)
    w0 = column(rw_ref[0:1, :], toks)
    w1 = column(rw_ref[1:2, :], toks)
    lane = lax.broadcasted_iota(jnp.int32, (toks, 128), 1)
    lower = (
        lax.broadcasted_iota(jnp.int32, (toks, toks), 0) > lax.broadcasted_iota(jnp.int32, (toks, toks), 1)
    ).astype(F32).astype(BF16)
    lane_e = (lane // 16).astype(F32)
    named_all = jnp.where((r0 == lane_e) | (r1 == lane_e), 1.0, 0.0)
    slot_all = mm(lower, named_all.astype(BF16))
    place_f = lax.rem(lane, 16).astype(F32)
    choose_all = jnp.where(slot_all + (4 * core).astype(F32) == place_f, named_all, 0.0).astype(BF16)
    mine = jnp.broadcast_to(s.astype(F32), (toks, 128))
    hit0 = jnp.where(r0 == mine, 1.0, 0.0)
    hit1 = jnp.where(r1 == mine, 1.0, 0.0)
    named = hit0 + hit1
    weight = hit0 * w0 + hit1 * w1
    slot = mm(lower, named.astype(BF16)) + (CAP * core).astype(F32)
    row_x = jnp.where(lane < 24, lane, -1).astype(F32)
    row_y = jnp.where(
        (lane >= 24) & (lane < 32), lane - 8, jnp.where((lane >= 32) & (lane < 48), lane - 32, -1)
    ).astype(F32)
    hot_x = jnp.where(slot == row_x, named, 0.0)
    hot_y = jnp.where(slot == row_y, named, 0.0)
    blank = jnp.zeros((128 - 2 * toks, 128), F32)
    hot = jnp.concatenate([hot_x, hot_y, blank], axis=0).T
    scale = jnp.concatenate([hot_x, hot_y * weight, blank], axis=0).T
    hot = hot[0:48, 0:48].astype(BF16)
    scale = jnp.sum(scale[0:48, :], axis=1, keepdims=True)
    for j in range(2 * nch):
        part = mm(hot, tok[:, j * kc : (j + 1) * kc]) * scale
        sb0[j] = part.astype(BF16)

    pl.semaphore_wait(barrier, 2 * NX - 1 + nz - 1 + 2 * (ns - 1))

    swap = rcopy(sb0.at[pl.ds(other * nch, nch)], rb, p0_s, p0_r, dev_c)
    swap.start()

    mix_f = mix_ref[...].astype(F32)
    mix_rows = jnp.concatenate([jnp.zeros((96, kc), F32), mix_f, jnp.zeros((8, kc), F32)], axis=0)
    PB[8:24] = mm(att1_ref[...], mix_rows.astype(BF16), NT)

    class Sum:
        def __init__(self, bufs, sems):
            self.part, self.g_in, self.z_in, self.full = bufs
            self.send, self.g_r, self.z_r, self.b_r = sems
            self.n8 = self.part.shape[2]

        def where(self, t):
            return t // (4 * self.n8), (t // self.n8) % 4, t % self.n8

        def put(self, t, tile):
            self.part[self.where(t)] = tile

        def get(self, t):
            return self.full[self.where(t)]

        def g_copy(self, m):
            dc, o = group[m]
            src = self.part.at[other if dc else core, lax.rem(xx + o, NX)]
            return rcopy(src, self.g_in.at[m], self.send.at[m], self.g_r.at[m], dev_g(dc, o))

        def z_copy(self, o):
            ref = self.z_in.at[zh]
            return rcopy(ref, ref, self.send.at[6 + o], self.z_r.at[o - 1], dev_z(o))

        def b_copy(self, m):
            ref = self.full.at[core, xx]
            return rcopy(ref, ref, self.send.at[10 + m], self.b_r.at[m], dev_g(*group[m]))

        def step(self, n):
            if n == 0:
                for m in range(7):
                    self.g_copy(m).start()
            elif n == 1:
                total = self.part[core, xx]
                for m in range(7):
                    self.g_copy(m).wait_recv()
                    total = total + self.g_in[m]
                self.z_in[zh] = total
                for o in range(1, 4):
                    self.z_copy(o).start()
            elif n == 2:
                for o in range(1, 4):
                    self.z_copy(o).wait_recv()
                self.full[core, xx] = self.z_in[0] + self.z_in[1] + self.z_in[2] + self.z_in[3]
                for m in range(7):
                    self.b_copy(m).start()
            else:
                for m in range(7):
                    self.b_copy(m).wait_recv()

        def sent(self):
            for m in range(7):
                self.g_copy(m).wait_send()
                self.b_copy(m).wait_send()
            for o in range(1, 4):
                self.z_copy(o).wait_send()

    att_sum = Sum(at_bufs, at_sems)
    back_sum = Sum(bk_bufs, bk_sems)

    acc_g[...] = jnp.zeros_like(acc_g)
    acc_u[...] = jnp.zeros_like(acc_u)
    acc_d[...] = jnp.zeros_like(acc_d)
    acc_l[...] = jnp.zeros_like(acc_l)

    swap.wait_recv()

    zm, zp, z2 = lax.rem(zh + 3, nz), lax.rem(zh + 1, nz), lax.rem(zh + 2, nz)
    dev_zp, dev_zm = dev_z(1), dev_z(3)
    last = nch - 1
    xs_of, zs_of = (xx, xm, xp, x2), (zh, zm, zp, z2)

    def along(k, first):
        return (k != last) == first

    def ring(k, on_z, fixed, which, ssem, rsem):
        ch = core * nch + k
        if on_z:
            at, low_, high_, up, down = fixed * nz + zh, fixed * nz + zm, fixed * nz + zp, dev_zp, dev_zm
        else:
            at, low_, high_, up, down = xx * nz + fixed, xm * nz + fixed, xp * nz + fixed, dev_xp, dev_xm
        if which == 0:
            ref, dev = G.at[ch, at], up
        elif which == 1:
            ref, dev = G.at[ch, at], down
        elif which == 2:
            ref, dev = G.at[ch, low_, :, pl.ds(0, kc // 2)], up
        else:
            ref, dev = G.at[ch, high_, :, pl.ds(kc // 2, kc // 2)], down
        return rcopy(ref, ref, ssem, rsem, dev)

    def s1(k, which):
        on_z = along(k, True)
        return ring(k, on_z, xx if on_z else zh, which, g_s.at[k], s1_r.at[k, which])

    def s2(k, p, which):
        on_z = along(k, False)
        fixed = xs_of[p] if on_z else zs_of[p]
        return ring(k, on_z, fixed, which, g_s.at[k], s2_r.at[k, p, which])

    def c_copy(k, p=None):
        if p is None:
            ref, n = G.at[core * nch + k], 0
        else:
            ref, n = G.at[core * nch + k, pl.ds(xs_of[p] * nz, nz)], p
        return rcopy(ref, ref, c_s.at[k, n], c_r.at[k, n], dev_c)

    def piece(k):
        G[core * nch + k, q] = (sb0[core * nch + k].astype(F32) + rb[k].astype(F32)).astype(BF16)

    def s2_out(k, p):
        s2(k, p, 0).start()
        s2(k, p, 1).start()

    def s1_pass(k):
        for which in range(2):
            s1(k, which).wait_recv()
            s1(k, 2 + which).start()
            if k != last:
                s2_out(k, 1 + which)

    def s1_far(k):
        s1(k, 2).wait_recv()
        s1(k, 3).wait_recv()
        s2_out(k, 3)

    def s2_pass(k, p):
        for which in range(2):
            s2(k, p, which).wait_recv()
            s2(k, p, 2 + which).start()

    def s2_done(k):
        for p in range(4):
            s2(k, p, 2).wait_recv()
            s2(k, p, 3).wait_recv()
            if k == last:
                c_copy(k, p).start()
        if k != last:
            c_copy(k).start()

    def product(ch):
        xrows = G[ch, :, 0:32, :].reshape(frame, kc)
        yrows = G[ch, :, 16:48, :].reshape(frame, kc)
        at = pl.ds(pl.multiple_of(ch * kc, kc), kc)
        acc_g[...] += mm(xrows, wg[at, :])
        acc_u[...] += mm(xrows, wu[at, :])
        acc_l[:, 0:16] += mm(xrows, a1[ch], NT)
        acc_d[...] += mm(yrows, wd[ch], NT)

    def of_other(k):
        if k == last:
            for p in range(4):
                c_copy(k, p).wait_recv()
        else:
            c_copy(k).wait_recv()
        product(other * nch + k)

    def s1_out(k):
        s1(k, 0).start()
        s1(k, 1).start()

    piece(last)
    s1_out(last)
    piece(0)
    s1_out(0)
    s2_out(0, 0)
    piece(1)
    s1_out(1)
    piece(2)
    s1_pass(last)
    s2_out(1, 0)
    s2_pass(0, 0)
    s1_pass(0)
    s1_out(2)
    s2_pass(1, 0)
    s1_pass(1)
    s1_far(0)
    s2_out(2, 0)
    s2_pass(0, 1)
    s2_pass(0, 2)
    s2_out(last, 0)
    s1_pass(2)
    s1_far(1)
    s2_out(last, 1)
    s2_pass(0, 3)
    s2_pass(2, 0)
    s1_far(2)
    s2_out(last, 2)
    s2_pass(1, 1)
    s2_pass(1, 2)
    s1_far(last)
    for copy in w_copies:
        copy.wait()
    s2_done(0)
    product(core * nch)
    s2_pass(last, 0)
    s2_pass(1, 3)
    s2_pass(last, 1)
    s2_pass(2, 1)
    s2_pass(2, 2)
    of_other(0)
    s2_done(1)
    product(core * nch + 1)
    s2_pass(last, 2)
    s2_pass(2, 3)
    s2_pass(last, 3)
    of_other(1)
    s2_done(2)
    product(core * nch + 2)
    of_other(2)
    s2_done(last)
    product(core * nch + last)
    of_other(last)

    low = acc_l[...].astype(BF16)
    gate = acc_g[...] + SCALE * mm(low[:, 0:16], a2_ref[...])
    hidden = gate.shape[1]
    gate = gate.reshape(chips, 32, hidden)[:, 0:24, :]
    upper = acc_u[...].reshape(chips, 32, hidden)[:, 0:24, :]
    dact = acc_d[...].reshape(chips, 32, hidden)
    dact = jnp.concatenate([dact[:, 16:32, :], dact[:, 8:16, :]], axis=1)
    sig = 1.0 / (1.0 + jnp.exp(-gate))
    dgate = dact * upper * sig * (1.0 + gate * (1.0 - sig))
    dup = dact * gate * sig
    du[...] = dup.reshape(rows, hidden).astype(BF16)
    dgate_rows = dgate.reshape(rows, hidden).astype(BF16)
    dg[...] = dgate_rows
    bk[...] = (SCALE * mm(dgate_rows, a2_ref[...], NT)).astype(BF16)
    dgate_frame = (
        jnp.concatenate([dgate, jnp.zeros((chips, 8, hidden), F32)], axis=1)
        .reshape(frame, hidden)
        .astype(BF16)
    )
    low_t = acc_l[...].T[0:16, :].astype(BF16)
    gs_ref[...] = SCALE * mm(low_t, dgate_frame)
    back_t = SCALE * mm(a2_ref[...], dgate_frame, NT)
    f_lanes = frame // 128
    n_back = 2 * f_lanes
    for j in range(n_back):
        r, l = j // f_lanes, j % f_lanes
        back_sum.put(j, back_t[r * 8 : r * 8 + 8, l * 128 : (l + 1) * 128])

    back_sum.step(0)

    slab = nz * 24
    half_slab = slab // 2

    hc = kc // 2

    def term(half, j):
        ch = half * nch + j // 2
        at = pl.ds(pl.multiple_of(ch * kc + (j % 2) * hc, hc), hc)
        cols = slice((j % 2) * hc, (j % 2) * hc + hc)
        return mm(dg[...], wg[at, :], NT) + mm(du[...], wu[at, :], NT) + mm(bk[...], a1[ch, :, cols])

    def t_copy(k):
        return rcopy(TB.at[k], TR.at[k], t_s.at[k], t_r.at[k], dev_c)

    def x1_copy(k, which):
        if which == 0:
            return rcopy(
                SB.at[k, x2, pl.ds(0, half_slab)], XR1.at[k, 0], x_s.at[k], x1_r.at[k, 0], dev_xp
            )
        return rcopy(
            SB.at[k, x2, pl.ds(half_slab, half_slab)], XR1.at[k, 1], x_s.at[k], x1_r.at[k, 1], dev_xm
        )

    def x2_copy(k, which):
        if which == 0:
            return rcopy(SB.at[k, xp], XR2.at[k, 0], x_s.at[k], x2_r.at[k, 0], dev_xp)
        return rcopy(SB.at[k, xm], XR2.at[k, 1], x_s.at[k], x2_r.at[k, 1], dev_xm)

    def zz_copy(k, o):
        return rcopy(ZB.at[k, zpeer(o)], ZR.at[k, o - 1], zz_s.at[k], zz_r.at[k, o - 1], dev_z(o))

    def e_copy(k, c_):
        return rcopy(EB.at[k, c_], E.at[s], e_s.at[k, c_], e_r.at[s], (dp_of(xx, zh, c_), core * nch + k))

    def e_local(k, c_):
        return pltpu.make_async_copy(EB.at[k, c_], E.at[s], e_l)

    def e_self(k, c_):
        return (core * nch + k == s) & (core == c_)

    def send_term(j):
        TB[j] = term(other, j).astype(BF16)
        t_copy(j).start()

    def core_sum(j):
        own = term(core, j)
        t_copy(j).wait_recv()
        SB[j] = (own + TR[j].astype(F32)).astype(BF16).reshape(NX, slab, hc)
        x1_copy(j, 0).start()
        x1_copy(j, 1).start()

    def x_pass(j):
        for which, there, at in ((0, xp, 0), (1, xm, half_slab)):
            x1_copy(j, which).wait_recv()
            SB[j, there, at : at + half_slab] = (
                SB[j, there, at : at + half_slab].astype(F32) + XR1[j, which].astype(F32)
            ).astype(BF16)
            x2_copy(j, which).start()

    def x_sum(j):
        x2_copy(j, 0).wait_recv()
        x2_copy(j, 1).wait_recv()
        return SB[j, xx].astype(F32) + XR2[j, 0].astype(F32) + XR2[j, 1].astype(F32)

    def z_send(k):
        left, right = x_sum(2 * k), x_sum(2 * k + 1)
        for z_ in range(nz):
            rows_ = slice(z_ * 24, z_ * 24 + 24)
            ZB[k, z_] = jnp.concatenate([left[rows_], right[rows_]], axis=0).astype(BF16)
        for o in range(1, nz):
            zz_copy(k, o).start()

    def z_sum(k):
        total = ZB[k, zh].astype(F32)
        for o in range(1, nz):
            zz_copy(k, o).wait_recv()
            total = total + ZR[k, o - 1].astype(F32)
        total = jnp.concatenate([total[0:24], total[24:48]], axis=1)
        EB[k, 0] = total[0:16].astype(BF16)
        EB[k, 1] = total[8:24].astype(BF16)
        for c_ in range(2):
            self_ = e_self(k, c_)

            @pl.when(self_)
            def _():
                e_local(k, c_).start()
                e_local(k, c_).wait()

            @pl.when(jnp.logical_not(self_))
            def _():
                e_copy(k, c_).start()

    send_term(0)
    for j in range(2 * nch + 8):
        if j + 1 < 2 * nch:
            send_term(j + 1)
        if j < 2 * nch:
            core_sum(j)
        if j in (2, 4):
            back_sum.step(j // 2)
        if 0 <= j - 2 < 2 * nch:
            x_pass(j - 2)
        at = j - 4
        if at % 2 == 1 and 0 <= at // 2 < nch:
            z_send(at // 2)
        at = j - 6
        if at % 2 == 1 and 0 <= at // 2 < nch:
            z_sum(at // 2)
    back_sum.step(3)

    def e_wait(o, carry):
        there = lax.rem(s + o, ns)
        rcopy(E.at[there], E.at[there], e_s.at[0, 0], e_r.at[there], dev_c).wait_recv()
        return carry

    lax.fori_loop(1, ns, e_wait, 0)
    home = s // nch == core

    @pl.when(jnp.logical_not(home))
    def _():
        rcopy(E.at[s], E.at[s], e_s.at[0, 0], e_r.at[s], dev_c).wait_recv()

    at = pl.ds(pl.multiple_of(s * kc, kc), kc)
    grad = mm(choose_all[:, 0 : 16 * ns], E[...].reshape(16 * ns, kc))
    spread = gain_ref[:, at] * grad
    hid_cols = hid_ref[:, at]
    hid_f = hid_cols.astype(F32)
    rad = rad_ref[:, 0:1]
    base = og_ref[:, at].astype(F32) + rad * spread
    stat_part = jnp.sum(spread * hid_f, axis=1, keepdims=True)
    PB[0:8, 0:toks] = jnp.broadcast_to(row_of(stat_part, toks), (8, toks))
    high, rest = two_parts(base)
    gap = jnp.zeros((8, kc), F32)
    stack = jnp.concatenate(
        [high.astype(F32), gap, rest.astype(F32), gap, hid_f, gap, jnp.zeros((32, kc), F32)], axis=0
    )
    PB[8:24] = PB[8:24] + mm(att2_ref[...], stack.astype(BF16), NT)

    def q_copy(o):
        return rcopy(PB, PR.at[o - 1], q_s, q_r.at[o - 1], (d, lax.rem(s + o, ns)))

    for o in range(1, ns):
        q_copy(o).start()
    total = PB[...]
    for o in range(1, ns):
        q_copy(o).wait_recv()
        total = total + PR[o - 1]
    stat_row = total[0:1, 0:toks] / width
    factor = rad * rad * rad * column(stat_row, toks)
    rg = (base - hid_f * factor).astype(BF16)
    rg_ref[...] = rg
    factor_row = row_of(factor, toks)
    low_parts = total[8:24, :]
    back_low = (
        low_parts[:, 0:toks] + low_parts[:, 32 : 32 + toks] - low_parts[:, 64 : 64 + toks] * factor_row
    ).astype(BF16)
    mixed_low = low_parts[:, 96 : 96 + toks].astype(BF16)
    first = SCALE * mm(back_low, mix_ref[...])
    second = SCALE * mm(mixed_low, rg)
    for j in range(lanes):
        cols = slice(j * 128, (j + 1) * 128)
        att_sum.put(j, first[0:8, cols])
        att_sum.put(lanes + j, first[8:16, cols])
        att_sum.put(2 * lanes + j, second[0:8, cols])
        att_sum.put(3 * lanes + j, second[8:16, cols])
    att_sum.step(0)

    back_full = jnp.concatenate(
        [
            jnp.concatenate([back_sum.get(r * f_lanes + l) for l in range(f_lanes)], axis=1)
            for r in range(2)
        ],
        axis=0,
    )
    high, rest = two_parts(back_full)
    both = jnp.concatenate([high, rest], axis=0)

    def first_gradient(ch, carry):
        xrows = G[ch, :, 0:32, :].reshape(frame, kc)
        pair = mm(both, xrows)
        ga_ref[:, pl.ds(pl.multiple_of(ch * kc, kc), kc)] = pair[0:16] + pair[16:32]
        return carry

    lax.fori_loop(0, 3, first_gradient, 0)
    att_sum.step(1)
    lax.fori_loop(3, 6, first_gradient, 0)
    att_sum.step(2)
    lax.fori_loop(6, 2 * nch, first_gradient, 0)

    swap.wait_send()

    def drain(k, carry):
        sent = G.at[k, pl.ds(0, 15)]
        rcopy(sent, sent, g_s.at[k], g_s.at[k], dev_c).wait_send()
        sent = ZB.at[k, pl.ds(0, nz - 1)]
        rcopy(sent, sent, zz_s.at[k], zz_s.at[k], dev_c).wait_send()
        for j in range(2):
            t_copy(2 * k + j).wait_send()
            sent = TB.at[2 * k + j, pl.ds(0, 3 * slab)]
            rcopy(sent, sent, x_s.at[2 * k + j], x_s.at[2 * k + j], dev_c).wait_send()
        for c_ in range(2):

            @pl.when(jnp.logical_not(e_self(k, c_)))
            def _():
                e_copy(k, c_).wait_send()

        return carry

    lax.fori_loop(0, nch, drain, 0)
    for k in range(last):
        c_copy(k).wait_send()
    for p in range(4):
        c_copy(last, p).wait_send()
    rcopy(PR, PR, q_s, q_s, dev_c).wait_send()
    back_sum.sent()

    att_sum.step(3)
    for j in range(lanes):
        cols = slice(j * 128, (j + 1) * 128)
        af_ref[0:8, cols] = att_sum.get(j)
        af_ref[8:16, cols] = att_sum.get(lanes + j)
        as_ref[0:8, cols] = att_sum.get(2 * lanes + j)
        as_ref[8:16, cols] = att_sum.get(3 * lanes + j)
    att_sum.sent()


def hand_on(*refs):
    count = len(refs) // 2
    for i in range(count):
        refs[count + i][...] = refs[i][...]


def fused(nz, ns, *args):
    hid, mix = args[0], args[1]
    width, kc = hid.shape[1], mix.shape[1]
    toks = hid.shape[0]
    hidden = args[6].shape[1]
    nch = ns // 2
    nd = NX * nz * 2
    chips = NX * nz
    rows, frame = chips * 24, chips * 32
    slab = nz * 24
    zo = max(nz - 1, 1)
    vm = pltpu.VMEM
    dma = pltpu.SemaphoreType.DMA
    sum_sems = (dma((17,)), dma((7,)), dma((3,)), dma((7,)))

    def tiles(count):
        n8 = count // 8
        return (
            vm((2, 4, n8, 8, 128), F32),
            vm((7, n8, 8, 128), F32),
            vm((4, n8, 8, 128), F32),
            vm((2, 4, n8, 8, 128), F32),
        )

    scratch = [
        vm((width, hidden), BF16),
        vm((width, hidden), BF16),
        vm((2 * nch, hidden, kc), BF16),
        vm((2 * nch, 16, kc), BF16),
        vm((nch, 48, kc), BF16),
        vm((2 * nch, 48, kc), BF16),
        vm((2 * nch, chips, 48, kc), BF16),
        vm((frame, hidden), F32),
        vm((frame, hidden), F32),
        vm((frame, hidden), F32),
        vm((frame, 128), F32),
        vm((rows, hidden), BF16),
        vm((rows, hidden), BF16),
        vm((rows, 16), BF16),
        vm((2 * nch, rows, kc // 2), BF16),
        vm((2 * nch, rows, kc // 2), BF16),
        vm((2 * nch, NX, slab, kc // 2), BF16),
        vm((2 * nch, 2, slab // 2, kc // 2), BF16),
        vm((2 * nch, 2, slab, kc // 2), BF16),
        vm((nch, nz, 48, kc // 2), BF16),
        vm((nch, zo, 48, kc // 2), BF16),
        vm((nch, 2, 16, kc), BF16),
        vm((ns, 16, kc), BF16),
        vm((24, 128), F32),
        vm((ns - 1, 24, 128), F32),
        tiles(4 * kc // 128),
        tiles(2 * frame // 128),
        vm((toks, 128), F32),
        dma((2 + 4 * nch,)),
        dma,
        dma,
        dma((nch,)),
        dma((nch, 4)),
        dma((nch, 4, 4)),
        dma((nch, 4)),
        dma((nch, 4)),
        dma((2 * nch,)),
        dma((2 * nch,)),
        dma((2 * nch,)),
        dma((2 * nch, 2)),
        dma((2 * nch, 2)),
        dma((nch,)),
        dma((nch, zo)),
        dma((nch, 2)),
        dma((ns,)),
        dma,
        dma,
        dma((ns - 1,)),
        sum_sems,
        sum_sems,
    ]
    vmem = pl.BlockSpec(memory_space=pltpu.VMEM)
    hbm = pl.BlockSpec(memory_space=pl.ANY)
    results = pl.pallas_call(
        functools.partial(kernel, nz, ns, kc),
        out_shape=(
            jax.ShapeDtypeStruct((toks, kc), BF16),
            jax.ShapeDtypeStruct((16, width), F32),
            jax.ShapeDtypeStruct((16, hidden), F32),
            jax.ShapeDtypeStruct((16, kc), F32),
            jax.ShapeDtypeStruct((16, kc), F32),
        ),
        in_specs=[vmem] * 6 + [hbm] * 4 + [vmem] * 3,
        out_specs=(vmem,) * 5,
        scratch_shapes=scratch,
        compiler_params=pltpu.CompilerParams(
            collective_id=0, has_side_effects=True, vmem_limit_bytes=58 * 1024 * 1024
        ),
        cost_estimate=pl.CostEstimate(
            flops=2 * rows * width * hidden * 5, bytes_accessed=6 * width * hidden, transcendentals=0
        ),
    )(*args)
    return pl.pallas_call(
        hand_on,
        out_shape=tuple(jax.ShapeDtypeStruct(r.shape, r.dtype) for r in results),
        in_specs=[vmem] * len(results),
        out_specs=(vmem,) * len(results),
    )(*results)


def body(nz, hid, mix, og, gain, routes, rw, wg, wu, wd, a1, a2, att1, att2):
    ns = lax.axis_size("shard")
    width, kc = hid.shape[1], mix.shape[1]
    rg, ga, gs, af, sec = fused(
        nz,
        ns,
        hid,
        mix,
        og,
        gain.reshape(1, width),
        routes.T,
        rw.T,
        wg[0],
        wu[0],
        wd[0],
        a1[0].T,
        a2[0],
        att1.T,
        att2,
    )
    return rg, ga.T[None], gs[None], af.T, sec


def solution(mesh):
    nz = mesh.shape["dp"] // (2 * NX)
    in_specs = (
        P("dp", None),
        P("dp", "shard"),
        P("dp", None),
        P(),
        P("dp", None),
        P("dp", None),
        P("shard", None, "dp"),
        P("shard", None, "dp"),
        P("shard", "dp", None),
        P("shard", None, None),
        P("shard", None, "dp"),
        P("shard", None),
        P(None, "shard"),
    )
    out_specs = (
        P("dp", "shard"),
        P("shard", None, None),
        P("shard", None, "dp"),
        P("shard", None),
        P(None, "shard"),
    )
    return jax.shard_map(
        functools.partial(body, nz), mesh=mesh, in_specs=in_specs, out_specs=out_specs, check_vma=False
    )
```

time: 142 us -> 116 us (0.82)
  Pallas kernels: 133 us -> 115 us
  local copies, waits for them, and re-layouts: 8.93 us -> 0 us
    pallas_call x1, Pallas kernels: 133 us -> 113 us  [fused(): pl.pallas_call(functools.partial(kernel, nz, ns, kc), out_shape=(jax.Shap...]
    unnamed x5 -> x0, local copies, waits for them, and re-layouts: 7.32 us -> none
    pallas_call x0 -> x1, Pallas kernels: none -> 1.81 us  [fused(): pl.pallas_call(hand_on, out_shape=tuple((jax.ShapeDtypeStruct(r.shape, r....]
    reshape x1 -> x0, local copies, waits for them, and re-layouts: 1.62 us -> none  [body(): a1_chunks = a1[0].T.reshape(16, ns, kc).swapaxes(0, 1)]
where the time goes in v2:
time: 116 us
  Pallas kernels  115 us (99%)
    pallas_call x1, Pallas kernels, fused(): pl.pallas_call(functools.partial(kernel, nz, ns, kc), out_shape=(jax.Shap...  113 us

profile of v2, /device:TPU:1, one launch (start us, length us, event | category | flops | bytes accessed | tf_op | source)
XLA Modules:
  0.0 115.9 jit_solution(5406175370973121087)
XLA Ops:
  0.6 113.5 %shard_map.164 = (bf16[24,768]{1,0:T(8,128)(2,1)}, f32[16,6144]{1,0:T(8,128)}, f32[16,256]{1,0:T(8,128)}, f32[16,768]{1,0:T(8,128)}, f32[16,768]{1,0:T(8,128)}) custom-call(bf16[24,6144]{1,0:T(8,128)(2,1)} %hid_ref.1, bf16[24,768]{1,0:T(8,128)(2,1)} %mix_ref.1, bf16[24,6144]{1,0:T(8,128)(2,1)} %og_ref.1, f32[1,6144]{1,0:T(1,128)} %bitcast.22, ...), custom_call_target="tpu_custom_call" | custom-call | flops 6039797760 | bytes 9437184 | tf_op jit(solution)/shard_map/pallas_call | solution.py:792
  114.1 1.8 %shard_map.165 = (bf16[24,768]{1,0:T(8,128)(2,1)}, f32[16,6144]{1,0:T(8,128)}, f32[16,256]{1,0:T(8,128)}, f32[16,768]{1,0:T(8,128)}, f32[16,768]{1,0:T(8,128)}) custom-call(bf16[24,768]{1,0:T(8,128)(2,1)} %get-tuple-element.15.refs_0_, f32[16,6144]{1,0:T(8,128)} %get-tuple-element.16.refs_1_, f32[16,256]{1,0:T(8,128)} %get-tuple-element.17.refs_2_, ...), custom_call_target="tpu_custom_call" | custom-call | tf_op jit(solution)/shard_map/pallas_call | solution.py:811

commit v3 on v2

--- a/solution.py
+++ b/solution.py
@@ -18,6 +18,28 @@
 NT = (((1,), (1,)), ((), ()))
 
 
+GATHER = (
+    ("I", 2), ("O", 2, 0), ("O", 0, 0), ("I", 3), ("O", 1, 0), ("I", 1), ("P1", 2, 0), ("P1", 2, 1),
+    ("P1", 1, 0), ("P1", 3, 1), ("P2", 1, 0, 0), ("P1", 3, 0), ("I", 0), ("O", 3, 2), ("P1", 1, 1), ("F1", 2),
+    ("F1", 3), ("F1", 1), ("P2", 2, 2, 1), ("P2", 2, 1, 1), ("P2", 2, 1, 0), ("O", 3, 1), ("P1", 0, 1),
+    ("P2", 2, 3, 0), ("P2", 1, 1, 0), ("P2", 1, 0, 1), ("P1", 0, 0), ("P2", 2, 2, 0), ("P2", 2, 0, 1),
+    ("O", 3, 3), ("P2", 2, 3, 1), ("O", 3, 0), ("P2", 1, 3, 1), ("P2", 1, 1, 1), ("P2", 1, 3, 0),
+    ("P2", 2, 0, 0), ("F1", 0), ("P2", 1, 2, 0), ("P2", 1, 2, 1), ("P2", 3, 2, 0), ("D", 2), ("P2", 3, 1, 1),
+    ("W", 2), ("P2", 0, 2, 0), ("P2", 0, 2, 1), ("P2", 3, 1, 0), ("P2", 3, 2, 1), ("P2", 0, 1, 0),
+    ("P2", 0, 0, 1), ("P2", 0, 0, 0), ("P2", 0, 1, 1), ("D", 1), ("P2", 0, 3, 1), ("P2", 3, 0, 1),
+    ("P2", 0, 3, 0), ("P2", 3, 0, 0), ("W", 1), ("T", 2), ("P2", 3, 3, 1), ("P2", 3, 3, 0), ("D", 0), ("T", 1),
+    ("W", 0), ("D", 3), ("W", 3), ("T", 0), ("T", 3),
+)
+REDUCE = (
+    ("P", 5), ("P", 4), ("P", 2), ("P", 3), ("A", 5), ("A", 4), ("A", 2), ("A", 3), ("B", 5, 1), ("B", 4, 0),
+    ("S", 1), ("P", 6), ("B", 4, 1), ("B", 5, 0), ("P", 0), ("P", 7), ("B", 3, 0), ("B", 2, 1), ("A", 6),
+    ("B", 2, 0), ("B", 3, 1), ("S", 2), ("A", 7), ("P", 1), ("A", 0), ("C", 2), ("B", 6, 0), ("B", 6, 1),
+    ("A", 1), ("S", 3), ("B", 7, 1), ("B", 7, 0), ("C", 1), ("G", 6), ("B", 0, 0), ("B", 0, 1), ("B", 1, 0),
+    ("B", 1, 1), ("D", 2), ("C", 3), ("G", 0), ("G", 4), ("C", 0), ("D", 1), ("G", 5), ("G", 1), ("G", 2),
+    ("D", 3), ("D", 0), ("G", 7), ("G", 3),
+)
+
+
 def mm(a, b, dims=NN):
     return lax.dot_general(a, b, dims, preferred_element_type=F32)
 
@@ -45,24 +67,28 @@
     nz,
     ns,
     kc,
-    hid_ref,
-    mix_ref,
-    og_ref,
-    gain_ref,
-    routes_ref,
-    rw_ref,
+    hid_hbm,
+    mix_hbm,
+    og_hbm,
+    gain_hbm,
+    routes_hbm,
+    rw_hbm,
     wg_hbm,
     wu_hbm,
     wd_hbm,
     a1_hbm,
-    a2_ref,
-    att1_ref,
-    att2_ref,
+    a2_hbm,
+    att1_hbm,
+    att2_hbm,
     rg_ref,
-    ga_ref,
+    ga_hbm,
     gs_ref,
     af_ref,
     as_ref,
+    small,
+    ga_ref,
+    ga_sem,
+    s_sem,
     wg,
     wu,
     wd,
@@ -114,6 +140,14 @@
     at_sems,
     bk_sems,
 ):
+    hid_ref, mix_ref, og_ref, gain_ref, routes_ref, rw_ref, a2_ref, att1_ref, att2_ref = small
+    small_hbm = (hid_hbm, mix_hbm, og_hbm, gain_hbm, routes_hbm, rw_hbm, a2_hbm, att1_hbm, att2_hbm)
+    s_copies = [
+        pltpu.make_async_copy(src, dst, s_sem.at[i]) for i, (src, dst) in enumerate(zip(small_hbm, small))
+    ]
+    for copy in s_copies:
+        copy.start()
+
     nch = ns // 2
     nd = NX * nz * 2
     chips = NX * nz
@@ -160,8 +194,6 @@
         pltpu.make_async_copy(a1_hbm.at[:, pl.ds(i * kc, kc)], a1.at[i], w_sem.at[2 + 2 * nch + i])
         for i in range(2 * nch)
     ]
-    for copy in w_copies:
-        copy.start()
 
     barrier = pltpu.get_barrier_semaphore()
 
@@ -185,6 +217,11 @@
         return carry
 
     lax.fori_loop(1, ns, greet_shard, 0)
+
+    for copy in w_copies:
+        copy.start()
+    for copy in s_copies:
+        copy.wait()
 
     hid = hid_ref[...].astype(F32)
     radius = lax.rsqrt(jnp.mean(hid * hid, axis=1, keepdims=True) + EPSILON)
@@ -349,23 +386,6 @@
         s2(k, p, 0).start()
         s2(k, p, 1).start()
 
-    def s1_pass(k):
-        for which in range(2):
-            s1(k, which).wait_recv()
-            s1(k, 2 + which).start()
-            if k != last:
-                s2_out(k, 1 + which)
-
-    def s1_far(k):
-        s1(k, 2).wait_recv()
-        s1(k, 3).wait_recv()
-        s2_out(k, 3)
-
-    def s2_pass(k, p):
-        for which in range(2):
-            s2(k, p, which).wait_recv()
-            s2(k, p, 2 + which).start()
-
     def s2_done(k):
         for p in range(4):
             s2(k, p, 2).wait_recv()
@@ -392,62 +412,43 @@
             c_copy(k).wait_recv()
         product(other * nch + k)
 
-    def s1_out(k):
-        s1(k, 0).start()
-        s1(k, 1).start()
-
-    piece(last)
-    s1_out(last)
-    piece(0)
-    s1_out(0)
-    s2_out(0, 0)
-    piece(1)
-    s1_out(1)
-    piece(2)
-    s1_pass(last)
-    s2_out(1, 0)
-    s2_pass(0, 0)
-    s1_pass(0)
-    s1_out(2)
-    s2_pass(1, 0)
-    s1_pass(1)
-    s1_far(0)
-    s2_out(2, 0)
-    s2_pass(0, 1)
-    s2_pass(0, 2)
-    s2_out(last, 0)
-    s1_pass(2)
-    s1_far(1)
-    s2_out(last, 1)
-    s2_pass(0, 3)
-    s2_pass(2, 0)
-    s1_far(2)
-    s2_out(last, 2)
-    s2_pass(1, 1)
-    s2_pass(1, 2)
-    s1_far(last)
-    for copy in w_copies:
-        copy.wait()
-    s2_done(0)
-    product(core * nch)
-    s2_pass(last, 0)
-    s2_pass(1, 3)
-    s2_pass(last, 1)
-    s2_pass(2, 1)
-    s2_pass(2, 2)
-    of_other(0)
-    s2_done(1)
-    product(core * nch + 1)
-    s2_pass(last, 2)
-    s2_pass(2, 3)
-    s2_pass(last, 3)
-    of_other(1)
-    s2_done(2)
-    product(core * nch + 2)
-    of_other(2)
-    s2_done(last)
-    product(core * nch + last)
-    of_other(last)
+    placed = set()
+    weights_here = False
+    for name, k, *rest in GATHER:
+        if name in ("I", "O") and k not in placed:
+            placed.add(k)
+            piece(k)
+        if name == "I":
+            s1(k, 0).start()
+            s1(k, 1).start()
+        elif name == "P1":
+            which = rest[0]
+            s1(k, which).wait_recv()
+            s1(k, 2 + which).start()
+            if k != last:
+                s2_out(k, 1 + which)
+        elif name == "F1":
+            s1(k, 2).wait_recv()
+            s1(k, 3).wait_recv()
+            if k != last:
+                s2_out(k, 3)
+        elif name == "O":
+            s2_out(k, rest[0])
+        elif name == "P2":
+            p, which = rest
+            s2(k, p, which).wait_recv()
+            s2(k, p, 2 + which).start()
+        elif name == "D":
+            s2_done(k)
+        else:
+            if not weights_here:
+                weights_here = True
+                for copy in w_copies:
+                    copy.wait()
+            if name == "W":
+                product(core * nch + k)
+            else:
+                of_other(k)
 
     low = acc_l[...].astype(BF16)
     gate = acc_g[...] + SCALE * mm(low[:, 0:16], a2_ref[...])
@@ -530,13 +531,13 @@
         x1_copy(j, 0).start()
         x1_copy(j, 1).start()
 
-    def x_pass(j):
-        for which, there, at in ((0, xp, 0), (1, xm, half_slab)):
-            x1_copy(j, which).wait_recv()
-            SB[j, there, at : at + half_slab] = (
-                SB[j, there, at : at + half_slab].astype(F32) + XR1[j, which].astype(F32)
-            ).astype(BF16)
-            x2_copy(j, which).start()
+    def x_pass(j, which):
+        there, at = ((xp, 0), (xm, half_slab))[which]
+        x1_copy(j, which).wait_recv()
+        SB[j, there, at : at + half_slab] = (
+            SB[j, there, at : at + half_slab].astype(F32) + XR1[j, which].astype(F32)
+        ).astype(BF16)
+        x2_copy(j, which).start()
 
     def x_sum(j):
         x2_copy(j, 0).wait_recv()
@@ -571,23 +572,42 @@
             def _():
                 e_copy(k, c_).start()
 
-    send_term(0)
-    for j in range(2 * nch + 8):
-        if j + 1 < 2 * nch:
-            send_term(j + 1)
-        if j < 2 * nch:
+    def back_parts():
+        back_full = jnp.concatenate(
+            [
+                jnp.concatenate([back_sum.get(r * f_lanes + l) for l in range(f_lanes)], axis=1)
+                for r in range(2)
+            ],
+            axis=0,
+        )
+        high, rest = two_parts(back_full)
+        both = jnp.concatenate([high, rest], axis=0)
+        return both
+
+    both, done = None, 0
+    ga_copy = pltpu.make_async_copy(ga_ref, ga_hbm, ga_sem)
+    for name, j, *rest in REDUCE:
+        if name == "P":
+            send_term(j)
+        elif name == "A":
             core_sum(j)
-        if j in (2, 4):
-            back_sum.step(j // 2)
-        if 0 <= j - 2 < 2 * nch:
-            x_pass(j - 2)
-        at = j - 4
-        if at % 2 == 1 and 0 <= at // 2 < nch:
-            z_send(at // 2)
-        at = j - 6
-        if at % 2 == 1 and 0 <= at // 2 < nch:
-            z_sum(at // 2)
-    back_sum.step(3)
+        elif name == "B":
+            x_pass(j, rest[0])
+        elif name == "C":
+            z_send(j)
+        elif name == "D":
+            z_sum(j)
+        elif name == "S":
+            back_sum.step(j)
+        else:
+            if both is None:
+                both = back_parts()
+            xrows = G[j, :, 0:32, :].reshape(frame, kc)
+            pair = mm(both, xrows)
+            ga_ref[:, j * kc : (j + 1) * kc] = pair[0:16] + pair[16:32]
+            done += 1
+            if done == 2 * nch:
+                ga_copy.start()
 
     def e_wait(o, carry):
         there = lax.rem(s + o, ns)
@@ -646,27 +666,8 @@
         att_sum.put(3 * lanes + j, second[8:16, cols])
     att_sum.step(0)
 
-    back_full = jnp.concatenate(
-        [
-            jnp.concatenate([back_sum.get(r * f_lanes + l) for l in range(f_lanes)], axis=1)
-            for r in range(2)
-        ],
-        axis=0,
-    )
-    high, rest = two_parts(back_full)
-    both = jnp.concatenate([high, rest], axis=0)
-
-    def first_gradient(ch, carry):
-        xrows = G[ch, :, 0:32, :].reshape(frame, kc)
-        pair = mm(both, xrows)
-        ga_ref[:, pl.ds(pl.multiple_of(ch * kc, kc), kc)] = pair[0:16] + pair[16:32]
-        return carry
-
-    lax.fori_loop(0, 3, first_gradient, 0)
     att_sum.step(1)
-    lax.fori_loop(3, 6, first_gradient, 0)
     att_sum.step(2)
-    lax.fori_loop(6, 2 * nch, first_gradient, 0)
 
     swap.wait_send()
 
@@ -703,6 +704,7 @@
         as_ref[0:8, cols] = att_sum.get(2 * lanes + j)
         as_ref[8:16, cols] = att_sum.get(3 * lanes + j)
     att_sum.sent()
+    ga_copy.wait()
 
 
 def hand_on(*refs):
@@ -736,6 +738,10 @@
         )
 
     scratch = [
+        tuple(vm(a.shape, a.dtype) for a in args[:6] + args[10:]),
+        vm((16, width), F32),
+        dma,
+        dma((9,)),
         vm((width, hidden), BF16),
         vm((width, hidden), BF16),
         vm((2 * nch, hidden, kc), BF16),
@@ -798,8 +804,8 @@
             jax.ShapeDtypeStruct((16, kc), F32),
             jax.ShapeDtypeStruct((16, kc), F32),
         ),
-        in_specs=[vmem] * 6 + [hbm] * 4 + [vmem] * 3,
-        out_specs=(vmem,) * 5,
+        in_specs=[hbm] * len(args),
+        out_specs=(vmem, hbm, vmem, vmem, vmem),
         scratch_shapes=scratch,
         compiler_params=pltpu.CompilerParams(
             collective_id=0, has_side_effects=True, vmem_limit_bytes=58 * 1024 * 1024

time: 116 us -> 114 us (0.983); the launches traced: 116 us -> 113 us
  Pallas kernels: 115 us -> 112 us
    pallas_call x1, Pallas kernels: 113 us -> 110 us  [fused(): pl.pallas_call(functools.partial(kernel, nz, ns, kc), out_shape=(jax.Shap...]
where the time goes in v3:
time: 114 us; the launch traced here: 113 us
  Pallas kernels  112 us (98%)
    pallas_call x1, Pallas kernels, fused(): pl.pallas_call(functools.partial(kernel, nz, ns, kc), out_shape=(jax.Shap...  110 us

profile of v3, /device:TPU:1, one launch (start us, length us, event | category | flops | bytes accessed | tf_op | source)
XLA Modules:
  0.0 112.7 jit_solution(4294033753033473505)
XLA Ops:
  0.6 110.2 %shard_map.164 = (bf16[24,768]{1,0:T(8,128)(2,1)}, f32[16,6144]{1,0:T(8,128)}, f32[16,256]{1,0:T(8,128)}, f32[16,768]{1,0:T(8,128)}, f32[16,768]{1,0:T(8,128)}) custom-call(bf16[24,6144]{1,0:T(8,128)(2,1)} %hid_hbm.1, bf16[24,768]{1,0:T(8,128)(2,1)} %mix_hbm.1, bf16[24,6144]{1,0:T(8,128)(2,1)} %og_hbm.1, f32[1,6144]{1,0:T(1,128)} %bitcast.22, ...), custom_call_target="tpu_custom_call" | custom-call | flops 6039797760 | bytes 9437184 | tf_op jit(solution)/shard_map/pallas_call | solution.py:798
  110.9 1.8 %shard_map.165 = (bf16[24,768]{1,0:T(8,128)(2,1)}, f32[16,6144]{1,0:T(8,128)}, f32[16,256]{1,0:T(8,128)}, f32[16,768]{1,0:T(8,128)}, f32[16,768]{1,0:T(8,128)}) custom-call(bf16[24,768]{1,0:T(8,128)(2,1)} %get-tuple-element.15.refs_0_, f32[16,6144]{1,0:T(8,128)} %get-tuple-element.16.refs_1_, f32[16,256]{1,0:T(8,128)} %get-tuple-element.17.refs_2_, ...), custom_call_target="tpu_custom_call" | custom-call | tf_op jit(solution)/shard_map/pallas_call | solution.py:817

commit v4 on v3

--- a/solution.py
+++ b/solution.py
@@ -145,9 +145,6 @@
     s_copies = [
         pltpu.make_async_copy(src, dst, s_sem.at[i]) for i, (src, dst) in enumerate(zip(small_hbm, small))
     ]
-    for copy in s_copies:
-        copy.start()
-
     nch = ns // 2
     nd = NX * nz * 2
     chips = NX * nz
@@ -218,6 +215,8 @@
 
     lax.fori_loop(1, ns, greet_shard, 0)
 
+    for copy in s_copies:
+        copy.start()
     for copy in w_copies:
         copy.start()
     for copy in s_copies:
@@ -609,6 +608,11 @@
             if done == 2 * nch:
                 ga_copy.start()
 
+    at = pl.ds(pl.multiple_of(s * kc, kc), kc)
+    hid_f = hid_ref[:, at].astype(F32)
+    og_f = og_ref[:, at].astype(F32)
+    gain_cols = gain_ref[:, at]
+    rad = rad_ref[:, 0:1]
     def e_wait(o, carry):
         there = lax.rem(s + o, ns)
         rcopy(E.at[there], E.at[there], e_s.at[0, 0], e_r.at[there], dev_c).wait_recv()
@@ -621,13 +625,9 @@
     def _():
         rcopy(E.at[s], E.at[s], e_s.at[0, 0], e_r.at[s], dev_c).wait_recv()
 
-    at = pl.ds(pl.multiple_of(s * kc, kc), kc)
     grad = mm(choose_all[:, 0 : 16 * ns], E[...].reshape(16 * ns, kc))
-    spread = gain_ref[:, at] * grad
-    hid_cols = hid_ref[:, at]
-    hid_f = hid_cols.astype(F32)
-    rad = rad_ref[:, 0:1]
-    base = og_ref[:, at].astype(F32) + rad * spread
+    spread = gain_cols * grad
+    base = og_f + rad * spread
     stat_part = jnp.sum(spread * hid_f, axis=1, keepdims=True)
     PB[0:8, 0:toks] = jnp.broadcast_to(row_of(stat_part, toks), (8, toks))
     high, rest = two_parts(base)

time: 114 us -> 115 us (level)
    pallas_call x1, Pallas kernels: 110 us -> 111 us  [fused(): pl.pallas_call(functools.partial(kernel, nz, ns, kc), out_shape=(jax.Shap...]
where the time goes in v4:
time: 115 us; the launch traced here: 114 us
  Pallas kernels  113 us (98%)
    pallas_call x1, Pallas kernels, fused(): pl.pallas_call(functools.partial(kernel, nz, ns, kc), out_shape=(jax.Shap...  111 us

profile of v4, /device:TPU:1, one launch (start us, length us, event | category | flops | bytes accessed | tf_op | source)
XLA Modules:
  0.0 113.9 jit_solution(14388474306377931232)
XLA Ops:
  0.6 111.5 %shard_map.164 = (bf16[24,768]{1,0:T(8,128)(2,1)}, f32[16,6144]{1,0:T(8,128)}, f32[16,256]{1,0:T(8,128)}, f32[16,768]{1,0:T(8,128)}, f32[16,768]{1,0:T(8,128)}) custom-call(bf16[24,6144]{1,0:T(8,128)(2,1)} %hid_hbm.1, bf16[24,768]{1,0:T(8,128)(2,1)} %mix_hbm.1, bf16[24,6144]{1,0:T(8,128)(2,1)} %og_hbm.1, f32[1,6144]{1,0:T(1,128)} %bitcast.22, ...), custom_call_target="tpu_custom_call" | custom-call | flops 6039797760 | bytes 9437184 | tf_op jit(solution)/shard_map/pallas_call | solution.py:798
  112.1 1.8 %shard_map.165 = (bf16[24,768]{1,0:T(8,128)(2,1)}, f32[16,6144]{1,0:T(8,128)}, f32[16,256]{1,0:T(8,128)}, f32[16,768]{1,0:T(8,128)}, f32[16,768]{1,0:T(8,128)}) custom-call(bf16[24,768]{1,0:T(8,128)(2,1)} %get-tuple-element.15.refs_0_, f32[16,6144]{1,0:T(8,128)} %get-tuple-element.16.refs_1_, f32[16,256]{1,0:T(8,128)} %get-tuple-element.17.refs_2_, ...), custom_call_target="tpu_custom_call" | custom-call | tf_op jit(solution)/shard_map/pallas_call | solution.py:817
